TPU v7x, 128 devices: a whole 4x4x4 slice. The times are simulated.
128 devices in a mesh: ctx: 16 (over y, x_hi, core), tp: 8 (over x_lo, z).
Axes of the slice: x: 4 (x_hi: 2, x_lo: 2; x = x_hi * 2 + x_lo), y: 4, z: 4, core: 2. Of those that a mesh axis runs over, the one named last changes fastest.
Arguments:
- query_proj: bfloat16 [16384, 8192], P('ctx', 'tp'), may hold values from -6 to 6
- key_proj: bfloat16 [16384, 8192], P('ctx', 'tp'), may hold values from -6 to 6
- value_proj: bfloat16 [16384, 8192], P('ctx', 'tp'), may hold values from -6 to 6
- cotangent: bfloat16 [16384, 8192], P('ctx', 'tp'), may hold values from -6 to 6
- short_taps: float32 [3, 3, 8192], P(None, None, 'tp'), may hold values from -2.5 to 2.5
- residues: float32 [512, 16], P('tp'), may hold values from -0.6 to 0.6
- decay_rates: float32 [512, 16], P('tp'), may hold values from 1.8310548e-05 to 0.08
Outputs:
- mixed: bfloat16 [16384, 8192], P('ctx', 'tp')
- grad_query: bfloat16 [16384, 8192], P('ctx', 'tp')
- grad_key: bfloat16 [16384, 8192], P('ctx', 'tp')
- grad_value: bfloat16 [16384, 8192], P('ctx', 'tp')
- grad_taps: float32 [3, 3, 8192], P(None, None, 'tp')
- grad_residues: float32 [512, 16], P('tp')
All inputs are finite; a program needn't handle non-finite values.
Results may differ from a plain program's by a relative error of at most 0.014.
Values may be sent and summed in bfloat16 or wider, within the bound.
A program may use at most 128 MiB of HBM per device.

v0:
```python
import functools

import jax
import jax.numpy as jnp
from jax import lax
from jax.experimental import pallas as pl
from jax.experimental.pallas import tpu as pltpu
from jax.sharding import PartitionSpec as P

BLK = 128
LANES = 128
MEM = 16
HI = lax.Precision.HIGHEST
F32 = jnp.float32
BF16 = jnp.bfloat16
MESH = pl.DeviceIdType.MESH


def lane_iota(rows):
    return lax.broadcasted_iota(jnp.int32, (rows, LANES), 1)


def row_iota(rows):
    return lax.broadcasted_iota(jnp.int32, (rows, LANES), 0)


def swap8(parts):
    piece = lane_iota(parts[0].shape[0]) // MEM
    for d in (4, 2, 1):
        high = (piece // d) % 2 == 1
        swapped = list(parts)
        for a in range(8):
            if a & d:
                continue
            low_part, high_part = parts[a], parts[a + d]
            swapped[a] = jnp.where(high, pltpu.roll(high_part, MEM * d, 1), low_part)
            swapped[a + d] = jnp.where(high, high_part, pltpu.roll(low_part, LANES - MEM * d, 1))
        parts = swapped
    return parts


def split(value):
    high = value.astype(BF16)
    low = (value - high.astype(F32)).astype(BF16)
    return high, low


def dot(a, b, dims=((1,), (0,))):
    return lax.dot_general(a, b, (dims, ((), ())), preferred_element_type=F32)


def column(table, g):
    return jnp.broadcast_to(table[:, MEM * g : MEM * g + 1], table.shape)


def kernel(
    n, tiles, halves, length, modes,
    query, key, value, cot, taps, rates, weights,
    mixed, grad_q, grad_k, grad_v, taps_out, res_out,
    inb, uf, ef, x3, g3, tf, tb, yv, zv, fs, gb, st, rs, halo, after, rn, wn, r3, w3, sout, gin,
    stage, tsum, trecv, gacc, grecv,
    in_sem, hs_sem, hr_sem, ss_sem, sr_sem, out_sem, ts_sem, tr_sem, gs_sem, gr_sem,
):
    me = lax.axis_index("ctx")
    blocks = length // BLK
    per = tiles // halves
    barrier = pltpu.get_barrier_semaphore()
    for d in range(1, n):
        pl.semaphore_signal(barrier, inc=1, device_id={"ctx": lax.rem(me + d, n)}, device_id_type=MESH)

    streams = (query, key, value, cot)

    def fetch(i, j):
        return pltpu.make_async_copy(
            streams[i].at[:, pl.ds(pl.multiple_of(j * LANES, LANES), LANES)], inb.at[i, j], in_sem.at[i, j]
        )

    for j in range(tiles):
        for i in range(4):
            fetch(i, j).start()

    group8 = (lane_iota(8) // MEM == row_iota(8)).astype(F32)
    repeat = (lane_iota(modes) % modes == row_iota(modes)).astype(F32)
    for j in range(tiles):
        rows = pl.ds(8 * j, 8)
        rn[j] = lax.dot_general(rates[rows, :], group8, (((0,), (0,)), ((), ())), precision=HI, preferred_element_type=F32)
        wn[j] = lax.dot_general(weights[rows, :], group8, (((0,), (0,)), ((), ())), precision=HI, preferred_element_type=F32)
    r3[...] = lax.dot_general(rates[...], repeat, (((1,), (0,)), ((), ())), precision=HI, preferred_element_type=F32)
    w3[...] = lax.dot_general(weights[...], repeat, (((1,), (0,)), ((), ())), precision=HI, preferred_element_type=F32)

    pl.semaphore_wait(barrier, n - 1)

    def behind(i):
        return pltpu.make_async_remote_copy(
            src_ref=streams[i].at[pl.ds(length - 16, 16), :], dst_ref=halo.at[i],
            send_sem=hs_sem.at[i], recv_sem=hr_sem.at[i],
            device_id={"ctx": lax.rem(me + 1, n)}, device_id_type=MESH,
        )

    def ahead(i):
        return pltpu.make_async_remote_copy(
            src_ref=streams[i].at[pl.ds(0, 16), :], dst_ref=after.at[i],
            send_sem=hs_sem.at[3 + i], recv_sem=hr_sem.at[3 + i],
            device_id={"ctx": lax.rem(me + n - 1, n)}, device_id_type=MESH,
        )

    for i in range(3):
        behind(i).start()
    for i in range(4):
        ahead(i).start()

    t_row = row_iota(BLK).astype(F32)
    lane_f = lane_iota(modes).astype(F32)
    lane_b = lane_iota(BLK)
    causal = row_iota(BLK) >= lane_iota(BLK)
    anti = row_iota(BLK) <= lane_iota(BLK)

    def build(j, _):
        rn_j = rn[j]
        for g in range(8):
            at = 8 * j + g
            r_row = r3[pl.ds(at, 1), :]
            w_row = w3[pl.ds(at, 1), :]
            r_col = column(rn_j, g)
            pad = jnp.zeros((LANES - 3 * modes, LANES), BF16)
            for ref, reach, peer, mask in (
                (tf, t_row + 1.0, lane_f + 1.0, causal),
                (tb, (BLK - 1.0) - t_row, (BLK - 1.0) - lane_f, anti),
            ):
                high, low = split(w_row * jnp.exp(-r_row * reach))
                zero = jnp.zeros_like(high)
                left = jnp.where(lane_b < 2 * modes, high, jnp.where(lane_b < 3 * modes, low, zero))
                v_high, v_low = split(jnp.exp(r_col * peer))
                right = jnp.concatenate([v_high, v_low, v_high, pad], axis=0)
                table = dot(left, right)
                ref[at, :, 0:BLK] = jnp.where(mask, table, 0.0).astype(BF16)
                ref[at, :, BLK : 2 * BLK] = left
        return 0

    lax.fori_loop(0, tiles, build, 0)

    for i in range(3):
        behind(i).wait()
    for i in range(4):
        ahead(i).wait()

    first = (me == 0)
    last = (me == n - 1)
    lane16 = lane_iota(modes)
    piece16 = lane16 // MEM

    def phase1(j, _):
        lanes = pl.ds(pl.multiple_of(j * LANES, LANES), LANES)
        for i in range(4):
            fetch(i, j).wait()
        for i in range(3):
            prior = halo[i, :, lanes].astype(F32)[8:16]
            uf[j, i, 0:8, :] = jnp.where(first, 0.0, prior)
            nxt = after[i, :, lanes].astype(F32)[0:8]
            uf[j, i, 8 + length : 16 + length, :] = jnp.where(last, 0.0, nxt)

        def widen(c, _):
            for i in range(3):
                rows = pl.ds(pl.multiple_of(c * 64, 64), 64)
                uf[j, i, pl.ds(pl.multiple_of(c * 64 + 8, 8), 64), :] = inb[i, j, rows, :].astype(F32)
            return 0

        lax.fori_loop(0, length // 64, widen, 0)
        tap = [[taps[i, l : l + 1, lanes] for l in range(3)] for i in range(3)]

        def gate(c, _):
            s0 = pl.multiple_of(c * 16, 16)
            xs, gs = [], []
            for b in range(8):
                base = pl.multiple_of(b * BLK + s0, 16)
                short = []
                for i in range(3):
                    view = uf.at[j, i, pl.ds(base, 24), :]
                    total = tap[i][0] * view[8:24, :] + tap[i][1] * view[7:23, :] + tap[i][2] * view[6:22, :]
                    short.append(total)
                xs.append(short[1] * short[2])
                gs.append(inb[3, j, pl.ds(base, 16), :].astype(F32) * short[0])
            for ref, parts in ((x3, xs), (g3, gs)):
                for g, part in enumerate(swap8(parts)):
                    ref[8 * j + g, pl.ds(s0, 16), :] = part.astype(BF16)
            return 0

        lax.fori_loop(0, BLK // 16, gate, 0)

        rn_j = rn[j]
        ahead_state = jnp.zeros((modes, LANES), F32)
        back_state = jnp.zeros((modes, LANES), F32)
        for g in range(8):
            at = 8 * j + g
            r_col = column(rn_j, g)
            absorb = jnp.concatenate(split(jnp.exp(-r_col * ((BLK - 1.0) - lane_f))), axis=0)
            ends2 = dot(absorb, x3[at, 0:BLK, :])
            ends = ends2[0:modes] + ends2[modes : 2 * modes]
            emit = jnp.concatenate(split(jnp.exp(-r_col * (lane_f + 1.0))), axis=0)
            starts2 = dot(emit, g3[at, 0:BLK, :])
            starts = starts2[0:modes] + starts2[modes : 2 * modes]
            gb[at] = starts
            power = jnp.exp(-r_col * float(BLK))
            for d in (1, 2, 4):
                moved = pltpu.roll(ends, MEM * d, 1)
                ends = ends + jnp.where(piece16 >= d, power * moved, 0.0)
                moved = pltpu.roll(starts, LANES - MEM * d, 1)
                starts = starts + jnp.where(piece16 < 8 - d, power * moved, 0.0)
                power = power * power
            ends_next = pltpu.roll(ends, MEM, 1)
            starts_prev = pltpu.roll(starts, LANES - MEM, 1)
            fs[0, at] = jnp.where(piece16 == 0, 0.0, ends_next)
            fs[1, at] = jnp.where(piece16 == 7, 0.0, starts_prev)
            place = pltpu.roll(ends_next, MEM * g, 1) if g else ends_next
            ahead_state = jnp.where(piece16 == g, place, ahead_state)
            place = pltpu.roll(starts, MEM * g, 1) if g else starts
            back_state = jnp.where(piece16 == g, place, back_state)
        st[j // per, 0, j % per] = ahead_state
        st[j // per, 1, j % per] = back_state
        return 0

    def send(h, d):
        return pltpu.make_async_remote_copy(
            src_ref=st.at[h, (me + d) // n], dst_ref=rs.at[h, d],
            send_sem=ss_sem.at[h, d], recv_sem=sr_sem.at[h, d],
            device_id={"ctx": lax.rem(me + d, n)}, device_id_type=MESH,
        )

    for h in range(halves):
        lax.fori_loop(h * per, (h + 1) * per, phase1, 0)
        for d in range(1, n):
            send(h, d).start()

    gacc[...] = jnp.zeros_like(gacc)

    def within(j, _):
        rn_j = rn[j]
        total = gacc[...]
        for g in range(8):
            at = 8 * j + g
            r_col = column(rn_j, g)
            pairs = dot(x3[at, 0:BLK, :], g3[at, 0:BLK, :], ((1,), (1,)))
            pairs = jnp.where(anti, pairs, 0.0).astype(BF16)
            rise = jnp.concatenate(split(jnp.exp(r_col * lane_f)), axis=0)
            both = dot(rise, pairs)
            terms = (both[0:modes] + both[modes : 2 * modes]) * jnp.exp(-r_col * lane_f)
            total = jnp.where(lane16 == at, total + jnp.sum(terms, axis=1, keepdims=True), total)
        gacc[...] = total
        return 0

    lax.fori_loop(0, tiles, within, 0)

    def combine(j, h):
        jj = j - h * per
        rn_j = rn[j]
        whole = jnp.exp(-rn_j * float(length))
        into = jnp.zeros((modes, LANES), F32)
        back = jnp.zeros((modes, LANES), F32)
        for e in range(n - 1, 0, -1):
            into = whole * into + jnp.where(e <= me, rs[h, e, jj], 0.0)
            back = whole * back + jnp.where(e <= n - 1 - me, rs[h, n - e, jj], 0.0)
        sout[j] = whole * into + st[h, 0, jj]
        gin[j] = back
        total = gacc[...]
        zeros = jnp.zeros((2 * BLK - BLK - 3 * modes, LANES), BF16)
        for g in range(8):
            at = 8 * j + g
            r_col = column(rn_j, g)
            here = []
            for state in (into, back):
                spread = jnp.where(piece16 == g, state, 0.0)
                for d in (1, 2, 4):
                    spread = spread + pltpu.roll(spread, MEM * d, 1)
                here.append(spread)
            step = piece16.astype(F32) * float(BLK)
            before = fs[0, at] + jnp.exp(-r_col * step) * here[0]
            behind_ = fs[1, at] + jnp.exp(-r_col * ((7.0 * BLK) - step)) * here[1]
            total = jnp.where(lane16 == at, total + jnp.sum(gb[at] * before, axis=1, keepdims=True), total)
            for ref, state in ((x3, before), (g3, behind_)):
                high, low = split(state)
                ref[at, BLK : 2 * BLK, :] = jnp.concatenate([high, low, high, zeros], axis=0)
        gacc[...] = total
        return h

    def put(i, j, slot):
        return pltpu.make_async_copy(
            stage.at[slot, i], (mixed, grad_q, grad_k, grad_v)[i].at[:, pl.ds(pl.multiple_of(j * LANES, LANES), LANES)],
            out_sem.at[slot, i],
        )

    def phase2(j, _):
        lanes = pl.ds(pl.multiple_of(j * LANES, LANES), LANES)
        slot = j % 2

        @pl.when(j >= 2)
        def _():
            for i in range(4):
                put(i, j - 2, slot).wait()

        for g in range(8):
            at = 8 * j + g
            yv[g] = dot(tf[at], x3[at])
            zv[g] = dot(tb[at], g3[at])
        tap = [[taps[i, l : l + 1, lanes] for l in range(3)] for i in range(3)]

        rn_j, wn_j = rn[j], wn[j]
        one = jnp.exp(rn_j)
        less = jnp.exp(-rn_j)

        def over(x):
            return jnp.sum(x, axis=0, keepdims=True)

        short = []
        for i in range(3):
            view = uf.at[j, i, length : length + 16, :]
            short.append(tap[i][0] * view[8:16, :] + tap[i][1] * view[7:15, :] + tap[i][2] * view[6:14, :])
        cot_next = jnp.where(last, 0.0, after[3, :, lanes].astype(F32)[0:8])
        x_next = (short[1] * short[2]).astype(BF16).astype(F32)[0:2]
        g_next = (cot_next * short[0]).astype(BF16).astype(F32)[0:1]
        h0 = over(wn_j)
        h1 = over(wn_j * less)
        long0 = over(wn_j * less * sout[j]) + h0 * x_next[0:1]
        long1 = over(wn_j * less * less * sout[j]) + h1 * x_next[0:1] + h0 * x_next[1:2]
        gg0 = over(wn_j * one * gin[j])
        gg1 = over(wn_j * one * one * gin[j]) - over(wn_j * one) * g_next
        row8 = row_iota(8)
        long_next = jnp.where(row8 == 0, long0, jnp.where(row8 == 1, long1, 0.0))
        gg_next = jnp.where(row8 == 0, gg0, jnp.where(row8 == 1, gg1, 0.0))
        ef[0, length : length + 8, :] = cot_next * long_next
        ef[1, length : length + 8, :] = gg_next * short[2]
        ef[2, length : length + 8, :] = gg_next * short[1]

        def finish(c, sums):
            s0 = pl.multiple_of(c * 16, 16)
            rows = pl.ds(s0, 16)
            longs = swap8([yv[g, rows, :] for g in range(8)])
            backs = swap8([zv[g, rows, :] for g in range(8)])
            sums = list(sums)
            for b in range(8):
                base = pl.multiple_of(b * BLK + s0, 16)
                short, windows = [], []
                for i in range(3):
                    view = uf.at[j, i, pl.ds(base, 24), :]
                    win = [view[8 - l : 24 - l, :] for l in range(3)]
                    windows.append(win)
                    short.append(tap[i][0] * win[0] + tap[i][1] * win[1] + tap[i][2] * win[2])
                stage[slot, 0, pl.ds(base, 16), :] = (short[0] * longs[b]).astype(BF16)
                grads = (
                    inb[3, j, pl.ds(base, 16), :].astype(F32) * longs[b],
                    backs[b] * short[2],
                    backs[b] * short[1],
                )
                for i in range(3):
                    ef[i, pl.ds(base, 16), :] = grads[i]
                    for l in range(3):
                        term = grads[i] * windows[i][l]
                        sums[3 * i + l] = sums[3 * i + l] + (term[0:8] + term[8:16])
            return tuple(sums)

        sums = lax.fori_loop(0, BLK // 16, finish, (jnp.zeros((8, LANES), F32),) * 9)
        for at in range(9):
            tsum[at : at + 1, lanes] = jnp.sum(sums[at], axis=0, keepdims=True)

        def spread(c, _):
            base = pl.multiple_of(c * 64, 64)
            for i in range(3):
                view = ef.at[i, pl.ds(base, 72), :]
                total = tap[i][0] * view[0:64, :] + tap[i][1] * view[1:65, :] + tap[i][2] * view[2:66, :]
                stage[slot, 1 + i, pl.ds(base, 64), :] = total.astype(BF16)
            return 0

        lax.fori_loop(0, length // 64, spread, 0)
        for i in range(4):
            put(i, j, slot).start()
        return 0

    for h in range(halves):
        for d in range(1, n):
            send(h, d).wait()
        lax.fori_loop(h * per, (h + 1) * per, combine, h)
        lax.fori_loop(h * per, (h + 1) * per, phase2, 0)

    tsum[9:16, :] = jnp.zeros((7, tsum.shape[1]), F32)
    trecv[me] = tsum[...].astype(BF16)
    grecv[me] = gacc[...]

    def give(d):
        peer = {"ctx": lax.rem(me + d, n)}
        return (
            pltpu.make_async_remote_copy(
                src_ref=trecv.at[me], dst_ref=trecv.at[me], send_sem=ts_sem.at[d], recv_sem=tr_sem.at[d],
                device_id=peer, device_id_type=MESH,
            ),
            pltpu.make_async_remote_copy(
                src_ref=grecv.at[me], dst_ref=grecv.at[me], send_sem=gs_sem.at[d], recv_sem=gr_sem.at[d],
                device_id=peer, device_id_type=MESH,
            ),
        )

    for d in range(1, n):
        for copy in give(d):
            copy.start()
    for j in range(max(0, tiles - 2), tiles):
        for i in range(4):
            put(i, j, j % 2).wait()
    for d in range(1, n):
        for copy in give(d):
            copy.wait()
    total = trecv[0].astype(F32)
    share = grecv[0]
    for s in range(1, n):
        total = total + trecv[s].astype(F32)
        share = share + grecv[s]
    taps_out[...] = total
    res_out[...] = share


def local(n, query, key, value, cot, taps, weights, rates):
    length, width = query.shape
    groups, modes = rates.shape
    tiles = width // LANES
    halves = 2 if tiles % 2 == 0 else 1
    per = tiles // halves
    big = jax.ShapeDtypeStruct((length, width), BF16)
    hbm = pl.BlockSpec(memory_space=pl.ANY)
    vmem = pl.BlockSpec(memory_space=pltpu.VMEM)
    dma = pltpu.SemaphoreType.DMA
    scratch = [
        pltpu.VMEM((4, tiles, length, LANES), BF16),
        pltpu.VMEM((tiles, 3, length + 16, LANES), F32),
        pltpu.VMEM((3, length + 8, LANES), F32),
        pltpu.VMEM((groups, 2 * BLK, LANES), BF16),
        pltpu.VMEM((groups, 2 * BLK, LANES), BF16),
        pltpu.VMEM((groups, BLK, 2 * LANES), BF16),
        pltpu.VMEM((groups, BLK, 2 * LANES), BF16),
        pltpu.VMEM((8, BLK, LANES), F32),
        pltpu.VMEM((8, BLK, LANES), F32),
        pltpu.VMEM((2, groups, modes, LANES), F32),
        pltpu.VMEM((groups, modes, LANES), F32),
        pltpu.VMEM((halves, 2, per, modes, LANES), F32),
        pltpu.VMEM((halves, n, per, modes, LANES), F32),
        pltpu.VMEM((3, 16, width), BF16),
        pltpu.VMEM((4, 16, width), BF16),
        pltpu.VMEM((tiles, modes, LANES), F32),
        pltpu.VMEM((tiles, modes, LANES), F32),
        pltpu.VMEM((groups, LANES), F32),
        pltpu.VMEM((groups, LANES), F32),
        pltpu.VMEM((tiles, modes, LANES), F32),
        pltpu.VMEM((tiles, modes, LANES), F32),
        pltpu.VMEM((2, 4, length, LANES), BF16),
        pltpu.VMEM((16, width), F32),
        pltpu.VMEM((n, 16, width), BF16),
        pltpu.VMEM((modes, LANES), F32),
        pltpu.VMEM((n, modes, LANES), F32),
        dma((4, tiles)), dma((7,)), dma((7,)), dma((halves, n)), dma((halves, n)), dma((2, 4)),
        dma((n,)), dma((n,)), dma((n,)), dma((n,)),
    ]
    mixed, grad_q, grad_k, grad_v, taps_sum, res_sum = pl.pallas_call(
        functools.partial(kernel, n, tiles, halves, length, modes),
        out_shape=(
            big, big, big, big,
            jax.ShapeDtypeStruct((16, width), F32),
            jax.ShapeDtypeStruct((modes, LANES), F32),
        ),
        in_specs=[hbm] * 4 + [vmem] * 3,
        out_specs=[hbm] * 4 + [vmem] * 2,
        scratch_shapes=scratch,
        compiler_params=pltpu.CompilerParams(
            collective_id=0, has_side_effects=True, vmem_limit_bytes=58 * 1024 * 1024
        ),
    )(query, key, value, cot, taps, rates, weights)
    grad_taps = taps_sum[:9].reshape(3, 3, width)
    return mixed, grad_q, grad_k, grad_v, grad_taps, res_sum[:, :groups].T


def solution(mesh):
    rows = P("ctx", "tp")
    n = mesh.shape["ctx"]
    return jax.shard_map(
        functools.partial(local, n),
        mesh=mesh,
        in_specs=(rows, rows, rows, rows, P(None, None, "tp"), P("tp", None), P("tp", None)),
        out_specs=(rows, rows, rows, rows, P(None, None, "tp"), P("tp", None)),
        check_vma=False,
    )
```

profile of v0, /device:TPU:1, one launch (start us, length us, event | category | flops | bytes accessed | tf_op | source)
XLA Modules:
  0.0 105.6 jit_solution(4056826441263500252)
XLA Ops:
  0.6 1.4 %copy.14.weights = f32[64,16]{1,0:T(8,128)} copy(f32[64,16]{0,1:T(8,128)} %param.12) | data formatting | bytes 8192 | tf_op args[5]
  2.0 1.4 %copy.13.rates = f32[64,16]{1,0:T(8,128)} copy(f32[64,16]{0,1:T(8,128)} %param.13) | data formatting | bytes 8192 | tf_op args[6]
  3.4 90.2 %shard_map.118 = (bf16[1024,1024]{1,0:T(8,128)(2,1)}, bf16[1024,1024]{1,0:T(8,128)(2,1)}, bf16[1024,1024]{1,0:T(8,128)(2,1)}, bf16[1024,1024]{1,0:T(8,128)(2,1)}, f32[16,1024]{1,0:T(8,128)}, /*index=5*/f32[16,128]{1,0:T(8,128)}) custom-call(bf16[1024,1024]{1,0:T(8,128)(2,1)} %query.1, bf16[1024,1024]{1,0:T(8,128)(2,1)} %key.1, bf16[1024,1024]{1,0:T(8,128)(2,1)} %value.1, ...), custom_call_target="tpu_custom_call" | custom-call | tf_op jit(solution)/shard_map/pallas_call | solution.py:458
  93.6 1.3 %slice_bitcast_fusion = f32[64,16]{0,1:T(8,128)} fusion(f32[16,128]{1,0:T(8,128)} %get-tuple-element.17), kind=kLoop, calls=%fused_computation | loop fusion | bytes 8192 | tf_op jit(solution)/shard_map/transpose | solution.py:473
  94.9 1.5 %reshape.15 = f32[3,3,1024]{2,1,0:T(4,128)} reshape(f32[9,1024]{1,0:T(8,128)} %bitcast.3) | data formatting | bytes 73728 | tf_op jit(solution)/shard_map/reshape | solution.py:472
  96.4 0.0 copy-start.2
  96.4 3.2 %copy.19 = bf16[1024,1024]{1,0:T(8,128)(2,1)} copy(bf16[1024,1024]{1,0:T(8,128)(2,1)} %get-tuple-element.24) | data formatting | bytes 4194304
  99.6 0.0 copy-done.2
  99.6 0.0 copy-start.1
  99.6 1.3 %copy.20 = bf16[1024,1024]{1,0:T(8,128)(2,1)} copy(bf16[1024,1024]{1,0:T(8,128)(2,1)S(1)} %copy-done.2) | data formatting | bytes 4194304
  100.9 1.0 copy-done.1
  101.9 0.0 copy-start
  101.9 1.3 %copy.21 = bf16[1024,1024]{1,0:T(8,128)(2,1)} copy(bf16[1024,1024]{1,0:T(8,128)(2,1)S(1)} %copy-done.1) | data formatting | bytes 4194304
  103.3 1.0 copy-done
  104.3 1.3 %copy.22 = bf16[1024,1024]{1,0:T(8,128)(2,1)} copy(bf16[1024,1024]{1,0:T(8,128)(2,1)S(1)} %copy-done) | data formatting | bytes 4194304
Async XLA Ops:
  96.4 3.2 %copy-start.2 = (bf16[1024,1024]{1,0:T(8,128)(2,1)S(1)}, bf16[1024,1024]{1,0:T(8,128)(2,1)}, u32[]{:S(2)}) copy-start(bf16[1024,1024]{1,0:T(8,128)(2,1)} %get-tuple-element.25) | copy-start | bytes 6291460
  99.6 2.3 %copy-start.1 = (bf16[1024,1024]{1,0:T(8,128)(2,1)S(1)}, bf16[1024,1024]{1,0:T(8,128)(2,1)}, u32[]{:S(2)}) copy-start(bf16[1024,1024]{1,0:T(8,128)(2,1)} %get-tuple-element.26) | copy-start | bytes 6291460
  101.9 2.3 %copy-start = (bf16[1024,1024]{1,0:T(8,128)(2,1)S(1)}, bf16[1024,1024]{1,0:T(8,128)(2,1)}, u32[]{:S(2)}) copy-start(bf16[1024,1024]{1,0:T(8,128)(2,1)} %get-tuple-element.27) | copy-start | bytes 6291460
where the time goes:
time: 106 us
  Pallas kernels  90.2 us (85%)
  local copies, waits for them, and re-layouts  14.8 us (14%)
    pallas_call x1, Pallas kernels, local(): pl.pallas_call(functools.partial(kernel, n, tiles, halves, length, modes)...  90.2 us
    unnamed x12, local copies, waits for them, and re-layouts  12 us

commit v1 on v0

v1 whole, which is shorter than its diff:
```python
import functools

import jax
import jax.numpy as jnp
from jax import lax
from jax.experimental import pallas as pl
from jax.experimental.pallas import tpu as pltpu
from jax.sharding import PartitionSpec as P

BLK = 128
LANES = 128
MEM = 16
HI = lax.Precision.HIGHEST
F32 = jnp.float32
BF16 = jnp.bfloat16
MESH = pl.DeviceIdType.MESH


def lane_iota(rows):
    return lax.broadcasted_iota(jnp.int32, (rows, LANES), 1)


def row_iota(rows):
    return lax.broadcasted_iota(jnp.int32, (rows, LANES), 0)


def turn(parts, piece):
    for d in (1, 2, 4):
        pick = (piece // d) % 2 == 1
        parts = [jnp.where(pick, parts[(g - d) % 8], parts[g]) for g in range(8)]
    return parts


def gather_groups(parts):
    piece = lane_iota(parts[0].shape[0]) // MEM
    parts = [pltpu.roll(p, MEM * b, 1) if b else p for b, p in enumerate(parts)]
    return turn([parts[-g % 8] for g in range(8)], piece)


def gather_blocks(parts):
    piece = lane_iota(parts[0].shape[0]) // MEM
    parts = turn([parts[-g % 8] for g in range(8)], piece)
    return [pltpu.roll(p, LANES - MEM * b, 1) if b else p for b, p in enumerate(parts)]


def split(value):
    high = value.astype(BF16)
    low = (value - high.astype(F32)).astype(BF16)
    return high, low


def dot(a, b, dims=((1,), (0,))):
    return lax.dot_general(a, b, (dims, ((), ())), preferred_element_type=F32)


def column(table, g):
    return jnp.broadcast_to(table[:, MEM * g : MEM * g + 1], table.shape)


def states_kernel(
    n, tiles, halves, length, modes,
    query, key, value, cot, taps, rates, weights,
    xs_out, gs_out, tf_out, tb_out, sf, sb, halo_out, after_out, rn, wn, sout, gin, gacc,
    inb, uf, xs, gs, tf, tb, fs, gb, st, rs, halo, after, r3, w3,
    in_sem, hs_sem, hr_sem, ss_sem, sr_sem, table_sem, part_sem,
):
    me = lax.axis_index("ctx")
    per = tiles // halves
    barrier = pltpu.get_barrier_semaphore()
    for d in range(1, n):
        pl.semaphore_signal(barrier, inc=1, device_id={"ctx": lax.rem(me + d, n)}, device_id_type=MESH)

    streams = (query, key, value, cot)

    def fetch(i, j):
        return pltpu.make_async_copy(
            streams[i].at[:, pl.ds(pl.multiple_of(j * LANES, LANES), LANES)], inb.at[i, j], in_sem.at[i, j]
        )

    for j in range(tiles):
        for i in range(4):
            fetch(i, j).start()

    def exact(a, b, dims):
        return lax.dot_general(a, b, (dims, ((), ())), precision=HI, preferred_element_type=F32)

    repeat = (lane_iota(modes) % modes == row_iota(modes)).astype(F32)
    for j in range(tiles):
        group = (lane_iota(8 * tiles) // MEM + 8 * j == row_iota(8 * tiles)).astype(F32)
        rn[j] = exact(rates[...], group, ((1,), (0,)))
        wn[j] = exact(weights[...], group, ((1,), (0,)))
    r3[...] = exact(rates[...], repeat, ((0,), (0,)))
    w3[...] = exact(weights[...], repeat, ((0,), (0,)))

    pl.semaphore_wait(barrier, n - 1)

    def behind(i):
        return pltpu.make_async_remote_copy(
            src_ref=streams[i].at[pl.ds(length - 16, 16), :], dst_ref=halo.at[i],
            send_sem=hs_sem.at[i], recv_sem=hr_sem.at[i],
            device_id={"ctx": lax.rem(me + 1, n)}, device_id_type=MESH,
        )

    def ahead(i):
        return pltpu.make_async_remote_copy(
            src_ref=streams[i].at[pl.ds(0, 16), :], dst_ref=after.at[i],
            send_sem=hs_sem.at[3 + i], recv_sem=hr_sem.at[3 + i],
            device_id={"ctx": lax.rem(me + n - 1, n)}, device_id_type=MESH,
        )

    for i in range(3):
        behind(i).start()
    for i in range(4):
        ahead(i).start()

    t_row = row_iota(BLK).astype(F32)
    lane_f = lane_iota(modes).astype(F32)
    lane_b = lane_iota(BLK)
    causal = row_iota(BLK) >= lane_iota(BLK)
    anti = row_iota(BLK) <= lane_iota(BLK)

    def build(j, _):
        rn_j = rn[j]
        for g in range(8):
            at = 8 * j + g
            r_row = r3[pl.ds(at, 1), :]
            w_row = w3[pl.ds(at, 1), :]
            r_col = column(rn_j, g)
            pad = jnp.zeros((LANES - 3 * modes, LANES), BF16)
            for ref, reach, peer, mask in (
                (tf, t_row + 1.0, lane_f + 1.0, causal),
                (tb, (BLK - 1.0) - t_row, (BLK - 1.0) - lane_f, anti),
            ):
                high, low = split(w_row * jnp.exp(-r_row * reach))
                zero = jnp.zeros_like(high)
                left = jnp.where(lane_b < 2 * modes, high, jnp.where(lane_b < 3 * modes, low, zero))
                v_high, v_low = split(jnp.exp(r_col * peer))
                right = jnp.concatenate([v_high, v_low, v_high, pad], axis=0)
                table = dot(left, right)
                ref[at, :, 0:BLK] = jnp.where(mask, table, 0.0).astype(BF16)
                ref[at, :, BLK : 2 * BLK] = left
        return 0

    lax.fori_loop(0, tiles, build, 0)
    tables = [
        pltpu.make_async_copy(source, target, table_sem.at[at])
        for at, (source, target) in enumerate(((tf, tf_out), (tb, tb_out)))
    ]
    for copy in tables:
        copy.start()

    for i in range(3):
        behind(i).wait()
    for i in range(4):
        ahead(i).wait()
    halo_out[...] = halo[...]
    after_out[...] = after[...]

    first = (me == 0)
    lane16 = lane_iota(modes)
    piece16 = lane16 // MEM

    def parts(j):
        rows = pl.ds(8 * j, 8)
        return [
            pltpu.make_async_copy(source.at[rows], target.at[rows], part_sem.at[at, j])
            for at, (source, target) in enumerate(((xs, xs_out), (gs, gs_out)))
        ]

    def phase1(j, _):
        lanes = pl.ds(pl.multiple_of(j * LANES, LANES), LANES)
        for i in range(4):
            fetch(i, j).wait()
        for i in range(3):
            prior = halo[i, :, lanes].astype(F32)[8:16]
            uf[i, 0:8, :] = jnp.where(first, 0.0, prior)

        def widen(c, _):
            for i in range(3):
                rows = pl.ds(pl.multiple_of(c * 64, 64), 64)
                uf[i, pl.ds(pl.multiple_of(c * 64 + 8, 8), 64), :] = inb[i, j, rows, :].astype(F32)
            return 0

        lax.fori_loop(0, length // 64, widen, 0)
        tap = [[taps[i, l : l + 1, lanes] for l in range(3)] for i in range(3)]

        def gate(c, _):
            s0 = pl.multiple_of(c * 16, 16)
            forward, backward = [], []
            for b in range(8):
                base = pl.multiple_of(b * BLK + s0, 16)
                short = []
                for i in range(3):
                    view = uf.at[i, pl.ds(base, 24), :]
                    total = tap[i][0] * view[8:24, :] + tap[i][1] * view[7:23, :] + tap[i][2] * view[6:22, :]
                    short.append(total)
                forward.append(short[1] * short[2])
                backward.append(inb[3, j, pl.ds(base, 16), :].astype(F32) * short[0])
            for ref, parts in ((xs, forward), (gs, backward)):
                for g, part in enumerate(gather_groups(parts)):
                    ref[8 * j + g, pl.ds(s0, 16), :] = part.astype(BF16)
            return 0

        lax.fori_loop(0, BLK // 16, gate, 0)

        rn_j = rn[j]
        ahead_state = jnp.zeros((modes, LANES), F32)
        back_state = jnp.zeros((modes, LANES), F32)
        for g in range(8):
            at = 8 * j + g
            r_col = column(rn_j, g)
            absorb = jnp.concatenate(split(jnp.exp(-r_col * ((BLK - 1.0) - lane_f))), axis=0)
            ends2 = dot(absorb, xs[at])
            ends = ends2[0:modes] + ends2[modes : 2 * modes]
            emit = jnp.concatenate(split(jnp.exp(-r_col * (lane_f + 1.0))), axis=0)
            starts2 = dot(emit, gs[at])
            starts = starts2[0:modes] + starts2[modes : 2 * modes]
            gb[at] = starts
            power = jnp.exp(-r_col * float(BLK))
            block = (piece16 + 8 - g) % 8
            for d in (1, 2, 4):
                moved = pltpu.roll(ends, MEM * d, 1)
                ends = ends + jnp.where(block >= d, power * moved, 0.0)
                moved = pltpu.roll(starts, LANES - MEM * d, 1)
                starts = starts + jnp.where(block < 8 - d, power * moved, 0.0)
                power = power * power
            ends_next = pltpu.roll(ends, MEM, 1)
            starts_prev = pltpu.roll(starts, LANES - MEM, 1)
            fs[0, at] = jnp.where(block == 0, 0.0, ends_next)
            fs[1, at] = jnp.where(block == 7, 0.0, starts_prev)
            ahead_state = jnp.where(piece16 == g, ends_next, ahead_state)
            back_state = jnp.where(piece16 == g, starts, back_state)
        st[j // per, 0, j % per] = ahead_state
        st[j // per, 1, j % per] = back_state
        for copy in parts(j):
            copy.start()
        return 0

    def send(h, d):
        return pltpu.make_async_remote_copy(
            src_ref=st.at[h, (me + d) // n], dst_ref=rs.at[h, d],
            send_sem=ss_sem.at[h, d], recv_sem=sr_sem.at[h, d],
            device_id={"ctx": lax.rem(me + d, n)}, device_id_type=MESH,
        )

    for h in range(halves):
        lax.fori_loop(h * per, (h + 1) * per, phase1, 0)
        for d in range(1, n):
            send(h, d).start()

    gacc[...] = jnp.zeros_like(gacc)

    def within(j, _):
        rn_j = rn[j]
        total = gacc[...]
        for g in range(8):
            at = 8 * j + g
            r_col = column(rn_j, g)
            pairs = dot(xs[at], gs[at].astype(F32).T.astype(BF16))
            pairs = jnp.where(anti, pairs, 0.0).astype(BF16)
            rise = jnp.concatenate(split(jnp.exp(r_col * lane_f)), axis=0)
            both = dot(rise, pairs)
            terms = (both[0:modes] + both[modes : 2 * modes]) * jnp.exp(-r_col * lane_f)
            total = jnp.where(lane16 == at, total + jnp.sum(terms, axis=1, keepdims=True), total)
        gacc[...] = total
        return 0

    lax.fori_loop(0, tiles, within, 0)

    def combine(j, h):
        jj = j - h * per
        rn_j = rn[j]
        whole = jnp.exp(-rn_j * float(length))
        into = jnp.zeros((modes, LANES), F32)
        back = jnp.zeros((modes, LANES), F32)
        for e in range(n - 1, 0, -1):
            into = whole * into + jnp.where(e <= me, rs[h, e, jj], 0.0)
            back = whole * back + jnp.where(e <= n - 1 - me, rs[h, n - e, jj], 0.0)
        sout[j] = whole * into + st[h, 0, jj]
        gin[j] = back
        total = gacc[...]
        for g in range(8):
            at = 8 * j + g
            r_col = column(rn_j, g)
            here = []
            for state in (into, back):
                spread = jnp.where(piece16 == g, state, 0.0)
                for d in (1, 2, 4):
                    spread = spread + pltpu.roll(spread, MEM * d, 1)
                here.append(spread)
            step = ((piece16 + 8 - g) % 8).astype(F32) * float(BLK)
            before = fs[0, at] + jnp.exp(-r_col * step) * here[0]
            behind_ = fs[1, at] + jnp.exp(-r_col * ((7.0 * BLK) - step)) * here[1]
            total = jnp.where(lane16 == at, total + jnp.sum(gb[at] * before, axis=1, keepdims=True), total)
            for ref, state in ((sf, before), (sb, behind_)):
                high, low = split(state)
                ref[at] = jnp.concatenate([high, low, high], axis=0)
        gacc[...] = total
        return h

    for h in range(halves):
        for d in range(1, n):
            send(h, d).wait()
        lax.fori_loop(h * per, (h + 1) * per, combine, h)
    for copy in tables:
        copy.wait()
    for j in range(tiles):
        for copy in parts(j):
            copy.wait()


def outputs_kernel(
    n, length, modes,
    query, key, value, cot, taps, xs, gs, tf, tb, sf, sb, halo, after, rn, wn, sout, gin,
    mixed, grad_q, grad_k, grad_v, tsum,
    uf, ef, yv, zv,
):
    first = lax.axis_index("ctx") == 0
    last = lax.axis_index("ctx") == n - 1
    for i in range(3):
        uf[i, 0:8, :] = jnp.where(first, 0.0, halo[i].astype(F32)[8:16])
        uf[i, 8 + length : 16 + length, :] = jnp.where(last, 0.0, after[i].astype(F32)[0:8])
    streams = (query, key, value)

    def widen(c, _):
        for i in range(3):
            rows = pl.ds(pl.multiple_of(c * 64, 64), 64)
            uf[i, pl.ds(pl.multiple_of(c * 64 + 8, 8), 64), :] = streams[i][rows, :].astype(F32)
        return 0

    lax.fori_loop(0, length // 64, widen, 0)
    zeros = jnp.zeros((BLK - 3 * modes, LANES), BF16)
    for g in range(8):
        yv[g] = dot(tf[g], jnp.concatenate([xs[g], sf[g], zeros], axis=0))
        zv[g] = dot(tb[g], jnp.concatenate([gs[g], sb[g], zeros], axis=0))
    tap = [[taps[i, l : l + 1, :] for l in range(3)] for i in range(3)]

    rn_j, wn_j = rn[0], wn[0]
    one = jnp.exp(rn_j)
    less = jnp.exp(-rn_j)

    def over(x):
        return jnp.sum(x, axis=0, keepdims=True)

    short = []
    for i in range(3):
        view = uf.at[i, length : length + 16, :]
        short.append(tap[i][0] * view[8:16, :] + tap[i][1] * view[7:15, :] + tap[i][2] * view[6:14, :])
    cot_next = jnp.where(last, 0.0, after[3].astype(F32)[0:8])
    x_next = (short[1] * short[2]).astype(BF16).astype(F32)[0:2]
    g_next = (cot_next * short[0]).astype(BF16).astype(F32)[0:1]
    h0 = over(wn_j)
    h1 = over(wn_j * less)
    long0 = over(wn_j * less * sout[0]) + h0 * x_next[0:1]
    long1 = over(wn_j * less * less * sout[0]) + h1 * x_next[0:1] + h0 * x_next[1:2]
    gg0 = over(wn_j * one * gin[0])
    gg1 = over(wn_j * one * one * gin[0]) - over(wn_j * one) * g_next
    row8 = row_iota(8)
    long_next = jnp.where(row8 == 0, long0, jnp.where(row8 == 1, long1, 0.0))
    gg_next = jnp.where(row8 == 0, gg0, jnp.where(row8 == 1, gg1, 0.0))
    ef[0, length : length + 8, :] = cot_next * long_next
    ef[1, length : length + 8, :] = gg_next * short[2]
    ef[2, length : length + 8, :] = gg_next * short[1]

    def finish(c, sums):
        s0 = pl.multiple_of(c * 16, 16)
        rows = pl.ds(s0, 16)
        longs = gather_blocks([yv[g, rows, :] for g in range(8)])
        backs = gather_blocks([zv[g, rows, :] for g in range(8)])
        sums = list(sums)
        for b in range(8):
            base = pl.multiple_of(b * BLK + s0, 16)
            short, windows = [], []
            for i in range(3):
                view = uf.at[i, pl.ds(base, 24), :]
                win = [view[8 - l : 24 - l, :] for l in range(3)]
                windows.append(win)
                short.append(tap[i][0] * win[0] + tap[i][1] * win[1] + tap[i][2] * win[2])
            mixed[pl.ds(base, 16), :] = (short[0] * longs[b]).astype(BF16)
            grads = (
                cot[pl.ds(base, 16), :].astype(F32) * longs[b],
                backs[b] * short[2],
                backs[b] * short[1],
            )
            for i in range(3):
                ef[i, pl.ds(base, 16), :] = grads[i]
                for l in range(3):
                    term = grads[i] * windows[i][l]
                    sums[3 * i + l] = sums[3 * i + l] + (term[0:8] + term[8:16])
        return tuple(sums)

    sums = lax.fori_loop(0, BLK // 16, finish, (jnp.zeros((8, LANES), F32),) * 9)
    for at in range(9):
        tsum[at : at + 1, :] = jnp.sum(sums[at], axis=0, keepdims=True)
    tsum[9:16, :] = jnp.zeros((7, LANES), F32)

    def spread(c, _):
        base = pl.multiple_of(c * 64, 64)
        for i in range(3):
            view = ef.at[i, pl.ds(base, 72), :]
            total = tap[i][0] * view[0:64, :] + tap[i][1] * view[1:65, :] + tap[i][2] * view[2:66, :]
            (grad_q, grad_k, grad_v)[i][pl.ds(base, 64), :] = total.astype(BF16)
        return 0

    lax.fori_loop(0, length // 64, spread, 0)


def sums_kernel(n, tiles, modes, tsum, gacc, taps_out, res_out, box, send_sem, recv_sem):
    me = lax.axis_index("ctx")
    barrier = pltpu.get_barrier_semaphore()
    for d in range(1, n):
        pl.semaphore_signal(barrier, inc=1, device_id={"ctx": lax.rem(me + d, n)}, device_id_type=MESH)
    for j in range(tiles):
        box[me, 16 * j : 16 * (j + 1), :] = tsum[:, LANES * j : LANES * (j + 1)].astype(BF16)
    high, low = split(gacc[...])
    box[me, 16 * tiles : 16 * tiles + modes, :] = high
    box[me, 16 * tiles + modes : 16 * tiles + 2 * modes, :] = low
    pl.semaphore_wait(barrier, n - 1)

    def give(d):
        return pltpu.make_async_remote_copy(
            src_ref=box.at[me], dst_ref=box.at[me], send_sem=send_sem.at[d], recv_sem=recv_sem.at[d],
            device_id={"ctx": lax.rem(me + d, n)}, device_id_type=MESH,
        )

    for d in range(1, n):
        give(d).start()
    for d in range(1, n):
        give(d).wait()
    total = box[0].astype(F32)
    for s in range(1, n):
        total = total + box[s].astype(F32)
    for j in range(tiles):
        taps_out[:, LANES * j : LANES * (j + 1)] = total[16 * j : 16 * (j + 1)]
    res_out[...] = total[16 * tiles : 16 * tiles + modes] + total[16 * tiles + modes :]


def local(n, query, key, value, cot, taps, weights, rates):
    length, width = query.shape
    groups, modes = rates.shape
    tiles = width // LANES
    halves = 2 if tiles % 2 == 0 else 1
    per = tiles // halves
    hbm = pl.BlockSpec(memory_space=pl.ANY)
    vmem = pl.BlockSpec(memory_space=pltpu.VMEM)
    dma = pltpu.SemaphoreType.DMA
    shape = jax.ShapeDtypeStruct
    natural = shape((tiles, modes, LANES), F32)
    part = shape((groups, BLK, LANES), BF16)
    table = shape((groups, BLK, 2 * LANES), BF16)
    carry = shape((groups, 3 * modes, LANES), BF16)
    *middle, gacc = pl.pallas_call(
        functools.partial(states_kernel, n, tiles, halves, length, modes),
        out_shape=(
            part, part, table, table, carry, carry,
            shape((3, 16, width), BF16), shape((4, 16, width), BF16),
            natural, natural, natural, natural, shape((modes, LANES), F32),
        ),
        in_specs=[hbm] * 4 + [vmem] * 3,
        out_specs=[hbm] * 4 + [vmem] * 9,
        scratch_shapes=[
            pltpu.VMEM((4, tiles, length, LANES), BF16),
            pltpu.VMEM((3, length + 16, LANES), F32),
            pltpu.VMEM((groups, BLK, LANES), BF16),
            pltpu.VMEM((groups, BLK, LANES), BF16),
            pltpu.VMEM((groups, BLK, 2 * LANES), BF16),
            pltpu.VMEM((groups, BLK, 2 * LANES), BF16),
            pltpu.VMEM((2, groups, modes, LANES), F32),
            pltpu.VMEM((groups, modes, LANES), F32),
            pltpu.VMEM((halves, 2, per, modes, LANES), F32),
            pltpu.VMEM((halves, n, per, modes, LANES), F32),
            pltpu.VMEM((3, 16, width), BF16),
            pltpu.VMEM((4, 16, width), BF16),
            pltpu.VMEM((groups, LANES), F32),
            pltpu.VMEM((groups, LANES), F32),
            dma((4, tiles)), dma((7,)), dma((7,)), dma((halves, n)), dma((halves, n)), dma((2,)), dma((2, tiles)),
        ],
        compiler_params=pltpu.CompilerParams(
            collective_id=0, has_side_effects=True, vmem_limit_bytes=60 * 1024 * 1024
        ),
    )(query, key, value, cot, taps, rates.T, weights.T)

    def stack(*shape):
        return pl.BlockSpec(shape, lambda j: (j, 0, 0))

    def wide(*shape):
        return pl.BlockSpec(shape, lambda j: (0, 0, j))

    tokens = pl.BlockSpec((length, LANES), lambda j: (0, j))
    big = shape((length, width), BF16)
    state = stack(1, modes, LANES)
    mixed, grad_q, grad_k, grad_v, tsum = pl.pallas_call(
        functools.partial(outputs_kernel, n, length, modes),
        grid=(tiles,),
        out_shape=(big, big, big, big, shape((16, width), F32)),
        in_specs=[
            tokens, tokens, tokens, tokens, wide(3, 3, LANES),
            stack(8, BLK, LANES), stack(8, BLK, LANES), stack(8, BLK, 2 * LANES), stack(8, BLK, 2 * LANES),
            stack(8, 3 * modes, LANES), stack(8, 3 * modes, LANES),
            wide(3, 16, LANES), wide(4, 16, LANES), state, state, state, state,
        ],
        out_specs=[tokens] * 4 + [pl.BlockSpec((16, LANES), lambda j: (0, j))],
        scratch_shapes=[
            pltpu.VMEM((3, length + 16, LANES), F32),
            pltpu.VMEM((3, length + 8, LANES), F32),
            pltpu.VMEM((8, BLK, LANES), F32),
            pltpu.VMEM((8, BLK, LANES), F32),
        ],
        compiler_params=pltpu.CompilerParams(
            dimension_semantics=("arbitrary",), vmem_limit_bytes=60 * 1024 * 1024
        ),
    )(query, key, value, cot, taps, *middle)
    rows = 16 * tiles + 2 * modes
    taps_sum, res_sum = pl.pallas_call(
        functools.partial(sums_kernel, n, tiles, modes),
        out_shape=(shape((16, width), F32), shape((modes, LANES), F32)),
        in_specs=[vmem] * 2,
        out_specs=[vmem] * 2,
        scratch_shapes=[pltpu.VMEM((n, rows, LANES), BF16), dma((n,)), dma((n,))],
        compiler_params=pltpu.CompilerParams(
            collective_id=1, has_side_effects=True, vmem_limit_bytes=60 * 1024 * 1024
        ),
    )(tsum, gacc)
    grad_taps = taps_sum[:9].reshape(3, 3, width)
    return mixed, grad_q, grad_k, grad_v, grad_taps, res_sum[:, :groups].T


def solution(mesh):
    rows = P("ctx", "tp")
    n = mesh.shape["ctx"]
    return jax.shard_map(
        functools.partial(local, n),
        mesh=mesh,
        in_specs=(rows, rows, rows, rows, P(None, None, "tp"), P("tp", None), P("tp", None)),
        out_specs=(rows, rows, rows, rows, P(None, None, "tp"), P("tp", None)),
        check_vma=False,
    )
```

time: 106 us -> 78.1 us (0.74)
  Pallas kernels: 90.2 us -> 74.3 us
  local copies, waits for them, and re-layouts: 14.8 us -> 2.77 us
    pallas_call x1 -> x3, Pallas kernels: 90.2 us -> 74.3 us  [the longest x1 39.7 us: local(): pl.pallas_call(functools.partial(states_kernel, n, tiles, halves, length,...]
    unnamed x12 -> x0, local copies, waits for them, and re-layouts: 12 us -> none
where the time goes in v1:
time: 78.1 us; the launch traced here: 77.7 us
  Pallas kernels  74.3 us (95%)
  local copies, waits for them, and re-layouts  2.77 us (4%)
    pallas_call x1, Pallas kernels, local(): pl.pallas_call(functools.partial(states_kernel, n, tiles, halves, length,...  39.7 us
    pallas_call x1, Pallas kernels, local(): pl.pallas_call(functools.partial(outputs_kernel, n, length, modes), grid=...  20.4 us
    pallas_call x1, Pallas kernels, local(): pl.pallas_call(functools.partial(sums_kernel, n, tiles, modes), out_shape...  14.2 us

profile of v1, /device:TPU:1, one launch (start us, length us, event | category | flops | bytes accessed | tf_op | source)
XLA Modules:
  0.0 77.7 jit_solution(7865690291190738326)
XLA Ops:
  0.6 39.7 %shard_map.118 = (bf16[64,128,128]{2,1,0:T(8,128)(2,1)}, bf16[64,128,128]{2,1,0:T(8,128)(2,1)}, bf16[64,128,256]{2,1,0:T(8,128)(2,1)}, bf16[64,128,256]{2,1,0:T(...) custom-call(bf16[1024,1024]{1,0:T(8,128)(2,1)} %query.3, ...), custom_call_target="tpu_custom_call" | custom-call | tf_op jit(solution)/shard_map/pallas_call | solution.py:452
  40.3 20.4 %shard_map.119 = (bf16[1024,1024]{1,0:T(8,128)(2,1)}, bf16[1024,1024]{1,0:T(8,128)(2,1)}, bf16[1024,1024]{1,0:T(8,128)(2,1)}, bf16[1024,1024]{1,0:T(8,128)(2,1)}, f32[16,1024]{1,0:T(8,128)}) custom-call(bf16[1024,1024]{1,0:T(8,128)(2,1)} %query.3, bf16[1024,1024]{1,0:T(8,128)(2,1)} %key.3, bf16[1024,1024]{1,0:T(8,128)(2,1)} %value.3, ...), custom_call_target="tpu_custom_call" | custom-call | tf_op jit(solution)/shard_map/pallas_call | solution.py:492
  60.7 14.2 %shard_map.120 = (f32[16,1024]{1,0:T(8,128)}, f32[16,128]{1,0:T(8,128)}) custom-call(f32[16,1024]{1,0:T(8,128)} %get-tuple-element.42.tsum, f32[16,128]{1,0:T(8,128)} %get-tuple-element.43.gacc), custom_call_target="tpu_custom_call" | custom-call | tf_op jit(solution)/shard_map/pallas_call | solution.py:514
  75.0 1.5 %reshape.15 = f32[3,3,1024]{2,1,0:T(4,128)} reshape(f32[9,1024]{1,0:T(8,128)} %bitcast.5) | data formatting | bytes 73728 | tf_op jit(solution)/shard_map/reshape | solution.py:524
  76.5 1.3 %slice_bitcast_fusion = f32[64,16]{0,1:T(8,128)} fusion(f32[16,128]{1,0:T(8,128)} %get-tuple-element.45), kind=kLoop, calls=%fused_computation | loop fusion | bytes 8192 | tf_op jit(solution)/shard_map/transpose | solution.py:525

commit v2 on v1

--- a/solution.py
+++ b/solution.py
@@ -57,13 +57,14 @@
     return jnp.broadcast_to(table[:, MEM * g : MEM * g + 1], table.shape)
 
 
-def states_kernel(
+def filters_kernel(
     n, tiles, halves, length, modes,
     query, key, value, cot, taps, rates, weights,
-    xs_out, gs_out, tf_out, tb_out, sf, sb, halo_out, after_out, rn, wn, sout, gin, gacc,
-    inb, uf, xs, gs, tf, tb, fs, gb, st, rs, halo, after, r3, w3,
-    in_sem, hs_sem, hr_sem, ss_sem, sr_sem, table_sem, part_sem,
+    long_out, back_out, halo_out, after_out, rn, wn, sout, gin, taps_out, res_out,
+    inb, uf, xs, gs, tf, tb, sf, sb, fs, gb, st, rs, halo, after, r3, w3, gacc, yv, zv, stage, tsum, *rest,
 ):
+    early, late = rest[0:2]
+    in_sem, hs_sem, hr_sem, ss_sem, sr_sem, out_sem, ts_sem, tr_sem = rest[2:]
     me = lax.axis_index("ctx")
     per = tiles // halves
     barrier = pltpu.get_barrier_semaphore()
@@ -91,27 +92,6 @@
         wn[j] = exact(weights[...], group, ((1,), (0,)))
     r3[...] = exact(rates[...], repeat, ((0,), (0,)))
     w3[...] = exact(weights[...], repeat, ((0,), (0,)))
-
-    pl.semaphore_wait(barrier, n - 1)
-
-    def behind(i):
-        return pltpu.make_async_remote_copy(
-            src_ref=streams[i].at[pl.ds(length - 16, 16), :], dst_ref=halo.at[i],
-            send_sem=hs_sem.at[i], recv_sem=hr_sem.at[i],
-            device_id={"ctx": lax.rem(me + 1, n)}, device_id_type=MESH,
-        )
-
-    def ahead(i):
-        return pltpu.make_async_remote_copy(
-            src_ref=streams[i].at[pl.ds(0, 16), :], dst_ref=after.at[i],
-            send_sem=hs_sem.at[3 + i], recv_sem=hr_sem.at[3 + i],
-            device_id={"ctx": lax.rem(me + n - 1, n)}, device_id_type=MESH,
-        )
-
-    for i in range(3):
-        behind(i).start()
-    for i in range(4):
-        ahead(i).start()
 
     t_row = row_iota(BLK).astype(F32)
     lane_f = lane_iota(modes).astype(F32)
@@ -141,13 +121,29 @@
                 ref[at, :, BLK : 2 * BLK] = left
         return 0
 
-    lax.fori_loop(0, tiles, build, 0)
-    tables = [
-        pltpu.make_async_copy(source, target, table_sem.at[at])
-        for at, (source, target) in enumerate(((tf, tf_out), (tb, tb_out)))
-    ]
-    for copy in tables:
-        copy.start()
+    lax.fori_loop(0, tiles // 2, build, 0)
+    pl.semaphore_wait(barrier, n - 1)
+
+    def behind(i):
+        return pltpu.make_async_remote_copy(
+            src_ref=streams[i].at[pl.ds(length - 16, 16), :], dst_ref=halo.at[i],
+            send_sem=hs_sem.at[i], recv_sem=hr_sem.at[i],
+            device_id={"ctx": lax.rem(me + 1, n)}, device_id_type=MESH,
+        )
+
+    def ahead(i):
+        return pltpu.make_async_remote_copy(
+            src_ref=streams[i].at[pl.ds(0, 16), :], dst_ref=after.at[i],
+            send_sem=hs_sem.at[3 + i], recv_sem=hr_sem.at[3 + i],
+            device_id={"ctx": lax.rem(me + n - 1, n)}, device_id_type=MESH,
+        )
+
+    for i in range(3):
+        behind(i).start()
+    for i in range(4):
+        ahead(i).start()
+
+    lax.fori_loop(tiles // 2, tiles, build, 0)
 
     for i in range(3):
         behind(i).wait()
@@ -160,25 +156,18 @@
     lane16 = lane_iota(modes)
     piece16 = lane16 // MEM
 
-    def parts(j):
-        rows = pl.ds(8 * j, 8)
-        return [
-            pltpu.make_async_copy(source.at[rows], target.at[rows], part_sem.at[at, j])
-            for at, (source, target) in enumerate(((xs, xs_out), (gs, gs_out)))
-        ]
-
     def phase1(j, _):
         lanes = pl.ds(pl.multiple_of(j * LANES, LANES), LANES)
         for i in range(4):
             fetch(i, j).wait()
         for i in range(3):
             prior = halo[i, :, lanes].astype(F32)[8:16]
-            uf[i, 0:8, :] = jnp.where(first, 0.0, prior)
+            uf[j, i, 0:8, :] = jnp.where(first, 0.0, prior)
 
         def widen(c, _):
             for i in range(3):
                 rows = pl.ds(pl.multiple_of(c * 64, 64), 64)
-                uf[i, pl.ds(pl.multiple_of(c * 64 + 8, 8), 64), :] = inb[i, j, rows, :].astype(F32)
+                uf[j, i, pl.ds(pl.multiple_of(c * 64 + 8, 8), 64), :] = inb[i, j, rows, :].astype(F32)
             return 0
 
         lax.fori_loop(0, length // 64, widen, 0)
@@ -191,7 +180,7 @@
                 base = pl.multiple_of(b * BLK + s0, 16)
                 short = []
                 for i in range(3):
-                    view = uf.at[i, pl.ds(base, 24), :]
+                    view = uf.at[j, i, pl.ds(base, 24), :]
                     total = tap[i][0] * view[8:24, :] + tap[i][1] * view[7:23, :] + tap[i][2] * view[6:22, :]
                     short.append(total)
                 forward.append(short[1] * short[2])
@@ -230,10 +219,8 @@
             fs[1, at] = jnp.where(block == 7, 0.0, starts_prev)
             ahead_state = jnp.where(piece16 == g, ends_next, ahead_state)
             back_state = jnp.where(piece16 == g, starts, back_state)
-        st[j // per, 0, j % per] = ahead_state
-        st[j // per, 1, j % per] = back_state
-        for copy in parts(j):
-            copy.start()
+        st[j // per, 0, j % per] = ahead_state.astype(BF16)
+        st[j // per, 1, j % per] = back_state.astype(BF16)
         return 0
 
     def send(h, d):
@@ -274,9 +261,9 @@
         into = jnp.zeros((modes, LANES), F32)
         back = jnp.zeros((modes, LANES), F32)
         for e in range(n - 1, 0, -1):
-            into = whole * into + jnp.where(e <= me, rs[h, e, jj], 0.0)
-            back = whole * back + jnp.where(e <= n - 1 - me, rs[h, n - e, jj], 0.0)
-        sout[j] = whole * into + st[h, 0, jj]
+            into = whole * into + jnp.where(e <= me, rs[h, e, jj].astype(F32), 0.0)
+            back = whole * back + jnp.where(e <= n - 1 - me, rs[h, n - e, jj].astype(F32), 0.0)
+        sout[j] = whole * into + st[h, 0, jj].astype(F32)
         gin[j] = back
         total = gacc[...]
         for g in range(8):
@@ -302,18 +289,107 @@
         for d in range(1, n):
             send(h, d).wait()
         lax.fori_loop(h * per, (h + 1) * per, combine, h)
-    for copy in tables:
-        copy.wait()
-    for j in range(tiles):
-        for copy in parts(j):
-            copy.wait()
+
+    def put(i, j, slot):
+        return pltpu.make_async_copy(stage.at[slot, i], (long_out, back_out)[i].at[j], out_sem.at[slot, i])
+
+    pad = jnp.zeros((BLK - 3 * modes, LANES), BF16)
+
+    def phase2(j, _):
+        lanes = pl.ds(pl.multiple_of(j * LANES, LANES), LANES)
+        slot = j % 2
+
+        @pl.when(j >= 2)
+        def _():
+            for i in range(2):
+                put(i, j - 2, slot).wait()
+
+        for g in range(8):
+            at = 8 * j + g
+            yv[g] = dot(tf[at], jnp.concatenate([xs[at], sf[at], pad], axis=0))
+            zv[g] = dot(tb[at], jnp.concatenate([gs[at], sb[at], pad], axis=0))
+        tap = [[taps[i, l : l + 1, lanes] for l in range(3)] for i in range(3)]
+
+        def finish(c, sums):
+            s0 = pl.multiple_of(c * 16, 16)
+            rows = pl.ds(s0, 16)
+            longs = gather_blocks([yv[g, rows, :] for g in range(8)])
+            backs = gather_blocks([zv[g, rows, :] for g in range(8)])
+            sums = list(sums)
+            for b in range(8):
+                base = pl.multiple_of(b * BLK + s0, 16)
+                stage[slot, 0, pl.ds(base, 16), :] = longs[b].astype(BF16)
+                stage[slot, 1, pl.ds(base, 16), :] = backs[b].astype(BF16)
+                short, windows = [], []
+                for i in range(3):
+                    view = uf.at[j, i, pl.ds(base, 24), :]
+                    win = [view[8 - l : 24 - l, :] for l in range(3)]
+                    windows.append(win)
+                    if i:
+                        short.append(tap[i][0] * win[0] + tap[i][1] * win[1] + tap[i][2] * win[2])
+                grads = (
+                    inb[3, j, pl.ds(base, 16), :].astype(F32) * longs[b],
+                    backs[b] * short[1],
+                    backs[b] * short[0],
+                )
+                for i in range(3):
+                    for l in range(3):
+                        term = grads[i] * windows[i][l]
+                        sums[3 * i + l] = sums[3 * i + l] + (term[0:8] + term[8:16])
+            return tuple(sums)
+
+        sums = lax.fori_loop(0, BLK // 16, finish, (jnp.zeros((8, LANES), F32),) * 9)
+        for at in range(9):
+            tsum[j, at : at + 1, :] = jnp.sum(sums[at], axis=0, keepdims=True)
+        tsum[j, 9:16, :] = jnp.zeros((7, LANES), F32)
+        for i in range(2):
+            put(i, j, slot).start()
+        return 0
+
+    def give(m, d):
+        box = (early, late)[m]
+        return pltpu.make_async_remote_copy(
+            src_ref=box.at[me], dst_ref=box.at[me], send_sem=ts_sem.at[m, d], recv_sem=tr_sem.at[m, d],
+            device_id={"ctx": lax.rem(me + d, n)}, device_id_type=MESH,
+        )
+
+    cut = max(0, tiles - 2)
+    for m, (lo, hi) in enumerate(((0, cut), (cut, tiles))):
+        lax.fori_loop(lo, hi, phase2, 0)
+        box = (early, late)[m]
+        base = 0
+        if m == 0:
+            high, low = split(gacc[...])
+            box[me, 0:modes, :] = high
+            box[me, modes : 2 * modes, :] = low
+            base = 2 * modes
+        for j in range(lo, hi):
+            box[me, base + 16 * (j - lo) : base + 16 * (j - lo + 1), :] = tsum[j].astype(BF16)
+        for d in range(1, n):
+            give(m, d).start()
+    for j in range(max(0, tiles - 2), tiles):
+        for i in range(2):
+            put(i, j, j % 2).wait()
+    for m, (lo, hi) in enumerate(((0, cut), (cut, tiles))):
+        for d in range(1, n):
+            give(m, d).wait()
+        box = (early, late)[m]
+        total = box[0].astype(F32)
+        for s in range(1, n):
+            total = total + box[s].astype(F32)
+        base = 0
+        if m == 0:
+            res_out[...] = total[0:modes] + total[modes : 2 * modes]
+            base = 2 * modes
+        for j in range(lo, hi):
+            taps_out[j] = total[base + 16 * (j - lo) : base + 16 * (j - lo + 1)]
 
 
 def outputs_kernel(
-    n, length, modes,
-    query, key, value, cot, taps, xs, gs, tf, tb, sf, sb, halo, after, rn, wn, sout, gin,
-    mixed, grad_q, grad_k, grad_v, tsum,
-    uf, ef, yv, zv,
+    n, length, groups,
+    query, key, value, cot, taps, long_low, back_low, halo, after, rn, wn, sout, gin, taps_sum, res_sum,
+    mixed, grad_q, grad_k, grad_v, grad_taps, grad_res,
+    uf, ef,
 ):
     first = lax.axis_index("ctx") == 0
     last = lax.axis_index("ctx") == n - 1
@@ -329,10 +405,6 @@
         return 0
 
     lax.fori_loop(0, length // 64, widen, 0)
-    zeros = jnp.zeros((BLK - 3 * modes, LANES), BF16)
-    for g in range(8):
-        yv[g] = dot(tf[g], jnp.concatenate([xs[g], sf[g], zeros], axis=0))
-        zv[g] = dot(tb[g], jnp.concatenate([gs[g], sb[g], zeros], axis=0))
     tap = [[taps[i, l : l + 1, :] for l in range(3)] for i in range(3)]
 
     rn_j, wn_j = rn[0], wn[0]
@@ -362,77 +434,31 @@
     ef[1, length : length + 8, :] = gg_next * short[2]
     ef[2, length : length + 8, :] = gg_next * short[1]
 
-    def finish(c, sums):
-        s0 = pl.multiple_of(c * 16, 16)
-        rows = pl.ds(s0, 16)
-        longs = gather_blocks([yv[g, rows, :] for g in range(8)])
-        backs = gather_blocks([zv[g, rows, :] for g in range(8)])
-        sums = list(sums)
-        for b in range(8):
-            base = pl.multiple_of(b * BLK + s0, 16)
-            short, windows = [], []
-            for i in range(3):
-                view = uf.at[i, pl.ds(base, 24), :]
-                win = [view[8 - l : 24 - l, :] for l in range(3)]
-                windows.append(win)
-                short.append(tap[i][0] * win[0] + tap[i][1] * win[1] + tap[i][2] * win[2])
-            mixed[pl.ds(base, 16), :] = (short[0] * longs[b]).astype(BF16)
-            grads = (
-                cot[pl.ds(base, 16), :].astype(F32) * longs[b],
-                backs[b] * short[2],
-                backs[b] * short[1],
-            )
-            for i in range(3):
-                ef[i, pl.ds(base, 16), :] = grads[i]
-                for l in range(3):
-                    term = grads[i] * windows[i][l]
-                    sums[3 * i + l] = sums[3 * i + l] + (term[0:8] + term[8:16])
-        return tuple(sums)
-
-    sums = lax.fori_loop(0, BLK // 16, finish, (jnp.zeros((8, LANES), F32),) * 9)
-    for at in range(9):
-        tsum[at : at + 1, :] = jnp.sum(sums[at], axis=0, keepdims=True)
-    tsum[9:16, :] = jnp.zeros((7, LANES), F32)
+    size = 32
 
     def spread(c, _):
-        base = pl.multiple_of(c * 64, 64)
+        base = pl.multiple_of(length - size - c * size, size)
+        rows = pl.ds(base, size)
+        short = []
         for i in range(3):
-            view = ef.at[i, pl.ds(base, 72), :]
-            total = tap[i][0] * view[0:64, :] + tap[i][1] * view[1:65, :] + tap[i][2] * view[2:66, :]
-            (grad_q, grad_k, grad_v)[i][pl.ds(base, 64), :] = total.astype(BF16)
+            view = uf.at[i, pl.ds(base, size + 8), :]
+            win = [view[8 - l : 8 + size - l, :] for l in range(3)]
+            short.append(tap[i][0] * win[0] + tap[i][1] * win[1] + tap[i][2] * win[2])
+        long_here = long_low[0, rows, :].astype(F32)
+        back_here = back_low[0, rows, :].astype(F32)
+        mixed[rows, :] = (short[0] * long_here).astype(BF16)
+        grads = (cot[rows, :].astype(F32) * long_here, back_here * short[2], back_here * short[1])
+        for i in range(3):
+            ef[i, rows, :] = grads[i]
+            view = ef.at[i, pl.ds(base, size + 8), :]
+            total = tap[i][0] * grads[i] + tap[i][1] * view[1 : 1 + size, :] + tap[i][2] * view[2 : 2 + size, :]
+            (grad_q, grad_k, grad_v)[i][rows, :] = total.astype(BF16)
         return 0
 
-    lax.fori_loop(0, length // 64, spread, 0)
-
-
-def sums_kernel(n, tiles, modes, tsum, gacc, taps_out, res_out, box, send_sem, recv_sem):
-    me = lax.axis_index("ctx")
-    barrier = pltpu.get_barrier_semaphore()
-    for d in range(1, n):
-        pl.semaphore_signal(barrier, inc=1, device_id={"ctx": lax.rem(me + d, n)}, device_id_type=MESH)
-    for j in range(tiles):
-        box[me, 16 * j : 16 * (j + 1), :] = tsum[:, LANES * j : LANES * (j + 1)].astype(BF16)
-    high, low = split(gacc[...])
-    box[me, 16 * tiles : 16 * tiles + modes, :] = high
-    box[me, 16 * tiles + modes : 16 * tiles + 2 * modes, :] = low
-    pl.semaphore_wait(barrier, n - 1)
-
-    def give(d):
-        return pltpu.make_async_remote_copy(
-            src_ref=box.at[me], dst_ref=box.at[me], send_sem=send_sem.at[d], recv_sem=recv_sem.at[d],
-            device_id={"ctx": lax.rem(me + d, n)}, device_id_type=MESH,
-        )
-
-    for d in range(1, n):
-        give(d).start()
-    for d in range(1, n):
-        give(d).wait()
-    total = box[0].astype(F32)
-    for s in range(1, n):
-        total = total + box[s].astype(F32)
-    for j in range(tiles):
-        taps_out[:, LANES * j : LANES * (j + 1)] = total[16 * j : 16 * (j + 1)]
-    res_out[...] = total[16 * tiles : 16 * tiles + modes] + total[16 * tiles + modes :]
+    lax.fori_loop(0, length // size, spread, 0)
+    for i in range(3):
+        grad_taps[i] = taps_sum[0, 3 * i : 3 * i + 3, :]
+    grad_res[...] = res_sum[:, 0:groups]
 
 
 def local(n, query, key, value, cot, taps, weights, rates):
@@ -441,39 +467,47 @@
     tiles = width // LANES
     halves = 2 if tiles % 2 == 0 else 1
     per = tiles // halves
+    cut = max(0, tiles - 2)
     hbm = pl.BlockSpec(memory_space=pl.ANY)
     vmem = pl.BlockSpec(memory_space=pltpu.VMEM)
     dma = pltpu.SemaphoreType.DMA
     shape = jax.ShapeDtypeStruct
     natural = shape((tiles, modes, LANES), F32)
-    part = shape((groups, BLK, LANES), BF16)
-    table = shape((groups, BLK, 2 * LANES), BF16)
-    carry = shape((groups, 3 * modes, LANES), BF16)
-    *middle, gacc = pl.pallas_call(
-        functools.partial(states_kernel, n, tiles, halves, length, modes),
+    tokens3 = shape((tiles, length, LANES), BF16)
+    middle = pl.pallas_call(
+        functools.partial(filters_kernel, n, tiles, halves, length, modes),
         out_shape=(
-            part, part, table, table, carry, carry,
-            shape((3, 16, width), BF16), shape((4, 16, width), BF16),
-            natural, natural, natural, natural, shape((modes, LANES), F32),
+            tokens3, tokens3, shape((3, 16, width), BF16), shape((4, 16, width), BF16),
+            natural, natural, natural, natural, shape((tiles, 16, LANES), F32), shape((modes, LANES), F32),
         ),
         in_specs=[hbm] * 4 + [vmem] * 3,
-        out_specs=[hbm] * 4 + [vmem] * 9,
+        out_specs=[hbm] * 2 + [vmem] * 8,
         scratch_shapes=[
             pltpu.VMEM((4, tiles, length, LANES), BF16),
-            pltpu.VMEM((3, length + 16, LANES), F32),
+            pltpu.VMEM((tiles, 3, length + 16, LANES), F32),
             pltpu.VMEM((groups, BLK, LANES), BF16),
             pltpu.VMEM((groups, BLK, LANES), BF16),
             pltpu.VMEM((groups, BLK, 2 * LANES), BF16),
             pltpu.VMEM((groups, BLK, 2 * LANES), BF16),
+            pltpu.VMEM((groups, 3 * modes, LANES), BF16),
+            pltpu.VMEM((groups, 3 * modes, LANES), BF16),
             pltpu.VMEM((2, groups, modes, LANES), F32),
             pltpu.VMEM((groups, modes, LANES), F32),
-            pltpu.VMEM((halves, 2, per, modes, LANES), F32),
-            pltpu.VMEM((halves, n, per, modes, LANES), F32),
+            pltpu.VMEM((halves, 2, per, modes, LANES), BF16),
+            pltpu.VMEM((halves, n, per, modes, LANES), BF16),
             pltpu.VMEM((3, 16, width), BF16),
             pltpu.VMEM((4, 16, width), BF16),
             pltpu.VMEM((groups, LANES), F32),
             pltpu.VMEM((groups, LANES), F32),
-            dma((4, tiles)), dma((7,)), dma((7,)), dma((halves, n)), dma((halves, n)), dma((2,)), dma((2, tiles)),
+            pltpu.VMEM((modes, LANES), F32),
+            pltpu.VMEM((8, BLK, LANES), F32),
+            pltpu.VMEM((8, BLK, LANES), F32),
+            pltpu.VMEM((2, 2, length, LANES), BF16),
+            pltpu.VMEM((tiles, 16, LANES), F32),
+            pltpu.VMEM((n, 2 * modes + 16 * cut, LANES), BF16),
+            pltpu.VMEM((n, 16 * (tiles - cut), LANES), BF16),
+            dma((4, tiles)), dma((7,)), dma((7,)), dma((halves, n)), dma((halves, n)), dma((2, 2)),
+            dma((2, n)), dma((2, n)),
         ],
         compiler_params=pltpu.CompilerParams(
             collective_id=0, has_side_effects=True, vmem_limit_bytes=60 * 1024 * 1024
@@ -489,40 +523,25 @@
     tokens = pl.BlockSpec((length, LANES), lambda j: (0, j))
     big = shape((length, width), BF16)
     state = stack(1, modes, LANES)
-    mixed, grad_q, grad_k, grad_v, tsum = pl.pallas_call(
-        functools.partial(outputs_kernel, n, length, modes),
+    *grads, grad_res = pl.pallas_call(
+        functools.partial(outputs_kernel, n, length, groups),
         grid=(tiles,),
-        out_shape=(big, big, big, big, shape((16, width), F32)),
+        out_shape=(big, big, big, big, shape((3, 3, width), F32), shape((modes, groups), F32)),
         in_specs=[
-            tokens, tokens, tokens, tokens, wide(3, 3, LANES),
-            stack(8, BLK, LANES), stack(8, BLK, LANES), stack(8, BLK, 2 * LANES), stack(8, BLK, 2 * LANES),
-            stack(8, 3 * modes, LANES), stack(8, 3 * modes, LANES),
-            wide(3, 16, LANES), wide(4, 16, LANES), state, state, state, state,
+            tokens, tokens, tokens, tokens, wide(3, 3, LANES), stack(1, length, LANES), stack(1, length, LANES),
+            wide(3, 16, LANES), wide(4, 16, LANES), state, state, state, state, stack(1, 16, LANES),
+            pl.BlockSpec((modes, LANES), lambda j: (0, 0)),
         ],
-        out_specs=[tokens] * 4 + [pl.BlockSpec((16, LANES), lambda j: (0, j))],
+        out_specs=[tokens] * 4 + [wide(3, 3, LANES), pl.BlockSpec((modes, groups), lambda j: (0, 0))],
         scratch_shapes=[
             pltpu.VMEM((3, length + 16, LANES), F32),
             pltpu.VMEM((3, length + 8, LANES), F32),
-            pltpu.VMEM((8, BLK, LANES), F32),
-            pltpu.VMEM((8, BLK, LANES), F32),
         ],
         compiler_params=pltpu.CompilerParams(
             dimension_semantics=("arbitrary",), vmem_limit_bytes=60 * 1024 * 1024
         ),
     )(query, key, value, cot, taps, *middle)
-    rows = 16 * tiles + 2 * modes
-    taps_sum, res_sum = pl.pallas_call(
-        functools.partial(sums_kernel, n, tiles, modes),
-        out_shape=(shape((16, width), F32), shape((modes, LANES), F32)),
-        in_specs=[vmem] * 2,
-        out_specs=[vmem] * 2,
-        scratch_shapes=[pltpu.VMEM((n, rows, LANES), BF16), dma((n,)), dma((n,))],
-        compiler_params=pltpu.CompilerParams(
-            collective_id=1, has_side_effects=True, vmem_limit_bytes=60 * 1024 * 1024
-        ),
-    )(tsum, gacc)
-    grad_taps = taps_sum[:9].reshape(3, 3, width)
-    return mixed, grad_q, grad_k, grad_v, grad_taps, res_sum[:, :groups].T
+    return (*grads, grad_res.T)
 
 
 def solution(mesh):

time: 78.1 us -> 73.6 us (0.942)
  local copies, waits for them, and re-layouts: 2.77 us -> 0 us
  Pallas kernels: 74.3 us -> 72.5 us
    pallas_call x3 -> x2, Pallas kernels: 74.3 us -> 72.5 us  [the longest x1 58.7 us: local(): pl.pallas_call(functools.partial(filters_kernel, n, tiles, halves, length...]
    reshape x1 -> x0, local copies, waits for them, and re-layouts: 1.48 us -> none  [local(): grad_taps = taps_sum[:9].reshape(3, 3, width)]
    transpose x1 -> x0, local copies, waits for them, and re-layouts: 1.29 us -> none  [local(): return (mixed, grad_q, grad_k, grad_v, grad_taps, res_sum[:, :groups].T)]
where the time goes in v2:
time: 73.6 us; the launch traced here: 73.2 us
  Pallas kernels  72.5 us (99%)
    pallas_call x1, Pallas kernels, local(): pl.pallas_call(functools.partial(filters_kernel, n, tiles, halves, length...  58.7 us
    pallas_call x1, Pallas kernels, local(): pl.pallas_call(functools.partial(outputs_kernel, n, length, groups), grid...  13.9 us

profile of v2, /device:TPU:1, one launch (start us, length us, event | category | flops | bytes accessed | tf_op | source)
XLA Modules:
  0.0 73.2 jit_solution(11874285293886946329)
XLA Ops:
  0.6 58.7 %shard_map.118 = (bf16[8,1024,128]{2,1,0:T(8,128)(2,1)}, bf16[8,1024,128]{2,1,0:T(8,128)(2,1)}, bf16[3,16,1024]{2,1,0:T(8,128)(2,1)}, bf16[4,16,1024]{2,1,0:T(8,...) custom-call(bf16[1024,1024]{1,0:T(8,128)(2,1)} %query.3, ...), custom_call_target="tpu_custom_call" | custom-call | tf_op jit(solution)/shard_map/pallas_call | solution.py:477
  59.3 13.9 %shard_map.119 = (bf16[1024,1024]{1,0:T(8,128)(2,1)}, bf16[1024,1024]{1,0:T(8,128)(2,1)}, bf16[1024,1024]{1,0:T(8,128)(2,1)}, bf16[1024,1024]{1,0:T(8,128)(2,1)}...) custom-call(bf16[1024,1024]{1,0:T(8,128)(2,1)} %query.3, bf16[1024,1024]{1,0:T(8,128)(2,1)} %key.3, bf16[1024,1024]{1,0:T(8,128)(2,1)} %value.3, ...), custom_call_target="tpu_custom_call" | custom-call | tf_op jit(solution)/shard_map/pallas_call | solution.py:526

commit v3 on v2

--- a/solution.py
+++ b/solution.py
@@ -61,7 +61,7 @@
     n, tiles, halves, length, modes,
     query, key, value, cot, taps, rates, weights,
     long_out, back_out, halo_out, after_out, rn, wn, sout, gin, taps_out, res_out,
-    inb, uf, xs, gs, tf, tb, sf, sb, fs, gb, st, rs, halo, after, r3, w3, gacc, yv, zv, stage, tsum, *rest,
+    inb, uf, xs, gs, tf, tb, sf, sb, fs, gb, st, rs, halo, after, r3, w3, gacc, yv, zv, stage, tsum, rc, *rest,
 ):
     early, late = rest[0:2]
     in_sem, hs_sem, hr_sem, ss_sem, sr_sem, out_sem, ts_sem, tr_sem = rest[2:]
@@ -106,6 +106,7 @@
             r_row = r3[pl.ds(at, 1), :]
             w_row = w3[pl.ds(at, 1), :]
             r_col = column(rn_j, g)
+            rc[at] = r_col
             pad = jnp.zeros((LANES - 3 * modes, LANES), BF16)
             for ref, reach, peer, mask in (
                 (tf, t_row + 1.0, lane_f + 1.0, causal),
@@ -145,6 +146,20 @@
 
     lax.fori_loop(tiles // 2, tiles, build, 0)
 
+    def arrive(j, _):
+        for i in range(4):
+            fetch(i, j).wait()
+
+        def widen(c, _):
+            for i in range(3):
+                rows = pl.ds(pl.multiple_of(c * 64, 64), 64)
+                uf[j, i, pl.ds(pl.multiple_of(c * 64 + 8, 8), 64), :] = inb[i, j, rows, :].astype(F32)
+            return 0
+
+        lax.fori_loop(0, length // 64, widen, 0)
+        return 0
+
+    lax.fori_loop(0, tiles, arrive, 0)
     for i in range(3):
         behind(i).wait()
     for i in range(4):
@@ -154,23 +169,13 @@
 
     first = (me == 0)
     lane16 = lane_iota(modes)
-    piece16 = lane16 // MEM
 
     def phase1(j, _):
         lanes = pl.ds(pl.multiple_of(j * LANES, LANES), LANES)
-        for i in range(4):
-            fetch(i, j).wait()
         for i in range(3):
             prior = halo[i, :, lanes].astype(F32)[8:16]
             uf[j, i, 0:8, :] = jnp.where(first, 0.0, prior)
 
-        def widen(c, _):
-            for i in range(3):
-                rows = pl.ds(pl.multiple_of(c * 64, 64), 64)
-                uf[j, i, pl.ds(pl.multiple_of(c * 64 + 8, 8), 64), :] = inb[i, j, rows, :].astype(F32)
-            return 0
-
-        lax.fori_loop(0, length // 64, widen, 0)
         tap = [[taps[i, l : l + 1, lanes] for l in range(3)] for i in range(3)]
 
         def gate(c, _):
@@ -192,33 +197,26 @@
 
         lax.fori_loop(0, BLK // 16, gate, 0)
 
-        rn_j = rn[j]
-        ahead_state = jnp.zeros((modes, LANES), F32)
-        back_state = jnp.zeros((modes, LANES), F32)
+        step = jnp.exp(-rn[j] * float(BLK))
+        ends, starts = [], []
         for g in range(8):
             at = 8 * j + g
-            r_col = column(rn_j, g)
+            r_col = rc[at]
             absorb = jnp.concatenate(split(jnp.exp(-r_col * ((BLK - 1.0) - lane_f))), axis=0)
-            ends2 = dot(absorb, xs[at])
-            ends = ends2[0:modes] + ends2[modes : 2 * modes]
+            both = dot(absorb, xs[at])
+            ends.append(both[0:modes] + both[modes : 2 * modes])
             emit = jnp.concatenate(split(jnp.exp(-r_col * (lane_f + 1.0))), axis=0)
-            starts2 = dot(emit, gs[at])
-            starts = starts2[0:modes] + starts2[modes : 2 * modes]
-            gb[at] = starts
-            power = jnp.exp(-r_col * float(BLK))
-            block = (piece16 + 8 - g) % 8
-            for d in (1, 2, 4):
-                moved = pltpu.roll(ends, MEM * d, 1)
-                ends = ends + jnp.where(block >= d, power * moved, 0.0)
-                moved = pltpu.roll(starts, LANES - MEM * d, 1)
-                starts = starts + jnp.where(block < 8 - d, power * moved, 0.0)
-                power = power * power
-            ends_next = pltpu.roll(ends, MEM, 1)
-            starts_prev = pltpu.roll(starts, LANES - MEM, 1)
-            fs[0, at] = jnp.where(block == 0, 0.0, ends_next)
-            fs[1, at] = jnp.where(block == 7, 0.0, starts_prev)
-            ahead_state = jnp.where(piece16 == g, ends_next, ahead_state)
-            back_state = jnp.where(piece16 == g, starts, back_state)
+            both = dot(emit, gs[at])
+            starts.append(both[0:modes] + both[modes : 2 * modes])
+        ends, starts = gather_blocks(ends), gather_blocks(starts)
+        ahead_state = back_state = jnp.zeros((modes, LANES), F32)
+        for b in range(8):
+            fs[0, j, b] = ahead_state
+            ahead_state = step * ahead_state + ends[b]
+            gb[j, b] = starts[b]
+        for b in range(7, -1, -1):
+            fs[1, j, b] = back_state
+            back_state = step * back_state + starts[b]
         st[j // per, 0, j % per] = ahead_state.astype(BF16)
         st[j // per, 1, j % per] = back_state.astype(BF16)
         return 0
@@ -240,15 +238,15 @@
     def within(j, _):
         rn_j = rn[j]
         total = gacc[...]
+        turned = [gs[8 * j + g].astype(F32).T.astype(BF16) for g in range(8)]
+        pairs = [dot(xs[8 * j + g], turned[g]) for g in range(8)]
+        pairs = [jnp.where(anti, p, 0.0).astype(BF16) for p in pairs]
         for g in range(8):
-            at = 8 * j + g
-            r_col = column(rn_j, g)
-            pairs = dot(xs[at], gs[at].astype(F32).T.astype(BF16))
-            pairs = jnp.where(anti, pairs, 0.0).astype(BF16)
+            r_col = rc[8 * j + g]
             rise = jnp.concatenate(split(jnp.exp(r_col * lane_f)), axis=0)
-            both = dot(rise, pairs)
+            both = dot(rise, pairs[g])
             terms = (both[0:modes] + both[modes : 2 * modes]) * jnp.exp(-r_col * lane_f)
-            total = jnp.where(lane16 == at, total + jnp.sum(terms, axis=1, keepdims=True), total)
+            total = jnp.where(lane16 == 8 * j + g, total + jnp.sum(terms, axis=1, keepdims=True), total)
         gacc[...] = total
         return 0
 
@@ -265,24 +263,23 @@
             back = whole * back + jnp.where(e <= n - 1 - me, rs[h, n - e, jj].astype(F32), 0.0)
         sout[j] = whole * into + st[h, 0, jj].astype(F32)
         gin[j] = back
-        total = gacc[...]
-        for g in range(8):
-            at = 8 * j + g
-            r_col = column(rn_j, g)
-            here = []
-            for state in (into, back):
-                spread = jnp.where(piece16 == g, state, 0.0)
-                for d in (1, 2, 4):
-                    spread = spread + pltpu.roll(spread, MEM * d, 1)
-                here.append(spread)
-            step = ((piece16 + 8 - g) % 8).astype(F32) * float(BLK)
-            before = fs[0, at] + jnp.exp(-r_col * step) * here[0]
-            behind_ = fs[1, at] + jnp.exp(-r_col * ((7.0 * BLK) - step)) * here[1]
-            total = jnp.where(lane16 == at, total + jnp.sum(gb[at] * before, axis=1, keepdims=True), total)
-            for ref, state in ((sf, before), (sb, behind_)):
+        step = jnp.exp(-rn_j * float(BLK))
+        reach_in, reach_back = into, back
+        before, behind_ = [None] * 8, [None] * 8
+        for b in range(8):
+            before[b] = fs[0, j, b] + reach_in
+            behind_[7 - b] = fs[1, j, 7 - b] + reach_back
+            reach_in = step * reach_in
+            reach_back = step * reach_back
+        terms = gb[j, 0] * before[0]
+        for b in range(1, 8):
+            terms = terms + gb[j, b] * before[b]
+        group = (row_iota(LANES) // MEM + 8 * j == lane_iota(LANES)).astype(F32)
+        gacc[...] += exact(terms, group, ((1,), (0,)))
+        for ref, blocks in ((sf, before), (sb, behind_)):
+            for g, state in enumerate(gather_groups(blocks)):
                 high, low = split(state)
-                ref[at] = jnp.concatenate([high, low, high], axis=0)
-        gacc[...] = total
+                ref[8 * j + g] = jnp.concatenate([high, low, high], axis=0)
         return h
 
     for h in range(halves):
@@ -318,8 +315,6 @@
             sums = list(sums)
             for b in range(8):
                 base = pl.multiple_of(b * BLK + s0, 16)
-                stage[slot, 0, pl.ds(base, 16), :] = longs[b].astype(BF16)
-                stage[slot, 1, pl.ds(base, 16), :] = backs[b].astype(BF16)
                 short, windows = [], []
                 for i in range(3):
                     view = uf.at[j, i, pl.ds(base, 24), :]
@@ -336,6 +331,10 @@
                     for l in range(3):
                         term = grads[i] * windows[i][l]
                         sums[3 * i + l] = sums[3 * i + l] + (term[0:8] + term[8:16])
+            for b in range(8):
+                rows = pl.ds(pl.multiple_of(b * BLK + s0, 16), 16)
+                stage[slot, 0, rows, :] = longs[b].astype(BF16)
+                stage[slot, 1, rows, :] = backs[b].astype(BF16)
             return tuple(sums)
 
         sums = lax.fori_loop(0, BLK // 16, finish, (jnp.zeros((8, LANES), F32),) * 9)
@@ -491,8 +490,8 @@
             pltpu.VMEM((groups, BLK, 2 * LANES), BF16),
             pltpu.VMEM((groups, 3 * modes, LANES), BF16),
             pltpu.VMEM((groups, 3 * modes, LANES), BF16),
-            pltpu.VMEM((2, groups, modes, LANES), F32),
-            pltpu.VMEM((groups, modes, LANES), F32),
+            pltpu.VMEM((2, tiles, 8, modes, LANES), F32),
+            pltpu.VMEM((tiles, 8, modes, LANES), F32),
             pltpu.VMEM((halves, 2, per, modes, LANES), BF16),
             pltpu.VMEM((halves, n, per, modes, LANES), BF16),
             pltpu.VMEM((3, 16, width), BF16),
@@ -504,6 +503,7 @@
             pltpu.VMEM((8, BLK, LANES), F32),
             pltpu.VMEM((2, 2, length, LANES), BF16),
             pltpu.VMEM((tiles, 16, LANES), F32),
+            pltpu.VMEM((groups, modes, LANES), F32),
             pltpu.VMEM((n, 2 * modes + 16 * cut, LANES), BF16),
             pltpu.VMEM((n, 16 * (tiles - cut), LANES), BF16),
             dma((4, tiles)), dma((7,)), dma((7,)), dma((halves, n)), dma((halves, n)), dma((2, 2)),

time: 73.6 us -> 66.9 us (0.909)
  Pallas kernels: 72.5 us -> 65.8 us
    pallas_call x1, Pallas kernels: 58.7 us -> 51.9 us  [local(): pl.pallas_call(functools.partial(filters_kernel, n, tiles, halves, length...]
where the time goes in v3:
time: 66.9 us; the launch traced here: 66.5 us
  Pallas kernels  65.8 us (98%)
    pallas_call x1, Pallas kernels, local(): pl.pallas_call(functools.partial(filters_kernel, n, tiles, halves, length...  51.9 us
    pallas_call x1, Pallas kernels, local(): pl.pallas_call(functools.partial(outputs_kernel, n, length, groups), grid...  13.9 us

profile of v3, /device:TPU:1, one launch (start us, length us, event | category | flops | bytes accessed | tf_op | source)
XLA Modules:
  0.0 66.5 jit_solution(3710538195682027380)
XLA Ops:
  0.6 51.9 %shard_map.118 = (bf16[8,1024,128]{2,1,0:T(8,128)(2,1)}, bf16[8,1024,128]{2,1,0:T(8,128)(2,1)}, bf16[3,16,1024]{2,1,0:T(8,128)(2,1)}, bf16[4,16,1024]{2,1,0:T(8,...) custom-call(bf16[1024,1024]{1,0:T(8,128)(2,1)} %query.3, ...), custom_call_target="tpu_custom_call" | custom-call | tf_op jit(solution)/shard_map/pallas_call | solution.py:476
  52.6 13.9 %shard_map.119 = (bf16[1024,1024]{1,0:T(8,128)(2,1)}, bf16[1024,1024]{1,0:T(8,128)(2,1)}, bf16[1024,1024]{1,0:T(8,128)(2,1)}, bf16[1024,1024]{1,0:T(8,128)(2,1)}...) custom-call(bf16[1024,1024]{1,0:T(8,128)(2,1)} %query.3, bf16[1024,1024]{1,0:T(8,128)(2,1)} %key.3, bf16[1024,1024]{1,0:T(8,128)(2,1)} %value.3, ...), custom_call_target="tpu_custom_call" | custom-call | tf_op jit(solution)/shard_map/pallas_call | solution.py:526

commit v4 on v3

--- a/solution.py
+++ b/solution.py
@@ -60,8 +60,8 @@
 def filters_kernel(
     n, tiles, halves, length, modes,
     query, key, value, cot, taps, rates, weights,
-    long_out, back_out, halo_out, after_out, rn, wn, sout, gin, taps_out, res_out,
-    inb, uf, xs, gs, tf, tb, sf, sb, fs, gb, st, rs, halo, after, r3, w3, gacc, yv, zv, stage, tsum, rc, *rest,
+    long_out, back_out, prior_out, next_out, taps_out, res_out,
+    inb, uf, xs, gs, tf, tb, sf, sb, fs, gb, st, rs, halo, after, r3, w3, gacc, yv, zv, stage, tsum, rc, rn, wn, sout, gin, *rest,
 ):
     early, late = rest[0:2]
     in_sem, hs_sem, hr_sem, ss_sem, sr_sem, out_sem, ts_sem, tr_sem = rest[2:]
@@ -160,22 +160,8 @@
         return 0
 
     lax.fori_loop(0, tiles, arrive, 0)
-    for i in range(3):
-        behind(i).wait()
-    for i in range(4):
-        ahead(i).wait()
-    halo_out[...] = halo[...]
-    after_out[...] = after[...]
-
-    first = (me == 0)
-    lane16 = lane_iota(modes)
-
-    def phase1(j, _):
+    def gate_of(j):
         lanes = pl.ds(pl.multiple_of(j * LANES, LANES), LANES)
-        for i in range(3):
-            prior = halo[i, :, lanes].astype(F32)[8:16]
-            uf[j, i, 0:8, :] = jnp.where(first, 0.0, prior)
-
         tap = [[taps[i, l : l + 1, lanes] for l in range(3)] for i in range(3)]
 
         def gate(c, _):
@@ -195,7 +181,32 @@
                     ref[8 * j + g, pl.ds(s0, 16), :] = part.astype(BF16)
             return 0
 
-        lax.fori_loop(0, BLK // 16, gate, 0)
+        return gate
+
+    def gates(j, _):
+        lax.fori_loop(1, BLK // 16, gate_of(j), 0)
+        return 0
+
+    lax.fori_loop(0, tiles, gates, 0)
+    for i in range(3):
+        behind(i).wait()
+    for i in range(4):
+        ahead(i).wait()
+
+    first = (me == 0)
+    last = (me == n - 1)
+    lane16 = lane_iota(modes)
+
+    def phase1(j, _):
+        lanes = pl.ds(pl.multiple_of(j * LANES, LANES), LANES)
+        for i in range(3):
+            prior = halo[i, :, lanes].astype(F32)[8:16]
+            prior = jnp.where(first, 0.0, prior)
+            uf[j, i, 0:8, :] = prior
+            prior_out[j, i] = prior
+            uf[j, i, 8 + length : 16 + length, :] = jnp.where(last, 0.0, after[i, :, lanes].astype(F32)[0:8])
+
+        lax.fori_loop(0, 1, gate_of(j), 0)
 
         step = jnp.exp(-rn[j] * float(BLK))
         ends, starts = [], []
@@ -282,10 +293,6 @@
                 ref[8 * j + g] = jnp.concatenate([high, low, high], axis=0)
         return h
 
-    for h in range(halves):
-        for d in range(1, n):
-            send(h, d).wait()
-        lax.fori_loop(h * per, (h + 1) * per, combine, h)
 
     def put(i, j, slot):
         return pltpu.make_async_copy(stage.at[slot, i], (long_out, back_out)[i].at[j], out_sem.at[slot, i])
@@ -352,9 +359,18 @@
             device_id={"ctx": lax.rem(me + d, n)}, device_id_type=MESH,
         )
 
+    def absorb_half(h):
+        for d in range(1, n):
+            send(h, d).wait()
+        lax.fori_loop(h * per, (h + 1) * per, combine, h)
+
     cut = max(0, tiles - 2)
+    absorb_half(0)
+    if halves == 2:
+        lax.fori_loop(0, min(per, cut), phase2, 0)
+        absorb_half(1)
     for m, (lo, hi) in enumerate(((0, cut), (cut, tiles))):
-        lax.fori_loop(lo, hi, phase2, 0)
+        lax.fori_loop(min(per, cut) if m == 0 else lo, hi, phase2, 0)
         box = (early, late)[m]
         base = 0
         if m == 0:
@@ -366,6 +382,39 @@
             box[me, base + 16 * (j - lo) : base + 16 * (j - lo + 1), :] = tsum[j].astype(BF16)
         for d in range(1, n):
             give(m, d).start()
+    def follow(j, _):
+        lanes = pl.ds(pl.multiple_of(j * LANES, LANES), LANES)
+        tap = [[taps[i, l : l + 1, lanes] for l in range(3)] for i in range(3)]
+
+        rn_j, wn_j = rn[j], wn[j]
+        one = jnp.exp(rn_j)
+        less = jnp.exp(-rn_j)
+
+        def over(x):
+            return jnp.sum(x, axis=0, keepdims=True)
+
+        short = []
+        for i in range(3):
+            view = uf.at[j, i, length : length + 16, :]
+            short.append(tap[i][0] * view[8:16, :] + tap[i][1] * view[7:15, :] + tap[i][2] * view[6:14, :])
+        cot_next = jnp.where(last, 0.0, after[3, :, lanes].astype(F32)[0:8])
+        x_next = (short[1] * short[2]).astype(BF16).astype(F32)[0:2]
+        g_next = (cot_next * short[0]).astype(BF16).astype(F32)[0:1]
+        h0 = over(wn_j)
+        h1 = over(wn_j * less)
+        long0 = over(wn_j * less * sout[j]) + h0 * x_next[0:1]
+        long1 = over(wn_j * less * less * sout[j]) + h1 * x_next[0:1] + h0 * x_next[1:2]
+        gg0 = over(wn_j * one * gin[j])
+        gg1 = over(wn_j * one * one * gin[j]) - over(wn_j * one) * g_next
+        row8 = row_iota(8)
+        long_next = jnp.where(row8 == 0, long0, jnp.where(row8 == 1, long1, 0.0))
+        gg_next = jnp.where(row8 == 0, gg0, jnp.where(row8 == 1, gg1, 0.0))
+        next_out[j, 0] = cot_next * long_next
+        next_out[j, 1] = gg_next * short[2]
+        next_out[j, 2] = gg_next * short[1]
+        return 0
+
+    lax.fori_loop(0, tiles, follow, 0)
     for j in range(max(0, tiles - 2), tiles):
         for i in range(2):
             put(i, j, j % 2).wait()
@@ -385,16 +434,14 @@
 
 
 def outputs_kernel(
-    n, length, groups,
-    query, key, value, cot, taps, long_low, back_low, halo, after, rn, wn, sout, gin, taps_sum, res_sum,
+    length, groups,
+    query, key, value, cot, taps, long_low, back_low, prior, following, taps_sum, res_sum,
     mixed, grad_q, grad_k, grad_v, grad_taps, grad_res,
     uf, ef,
 ):
-    first = lax.axis_index("ctx") == 0
-    last = lax.axis_index("ctx") == n - 1
     for i in range(3):
-        uf[i, 0:8, :] = jnp.where(first, 0.0, halo[i].astype(F32)[8:16])
-        uf[i, 8 + length : 16 + length, :] = jnp.where(last, 0.0, after[i].astype(F32)[0:8])
+        uf[i, 0:8, :] = prior[0, i]
+        ef[i, length : length + 8, :] = following[0, i]
     streams = (query, key, value)
 
     def widen(c, _):
@@ -406,34 +453,7 @@
     lax.fori_loop(0, length // 64, widen, 0)
     tap = [[taps[i, l : l + 1, :] for l in range(3)] for i in range(3)]
 
-    rn_j, wn_j = rn[0], wn[0]
-    one = jnp.exp(rn_j)
-    less = jnp.exp(-rn_j)
-
-    def over(x):
-        return jnp.sum(x, axis=0, keepdims=True)
-
-    short = []
-    for i in range(3):
-        view = uf.at[i, length : length + 16, :]
-        short.append(tap[i][0] * view[8:16, :] + tap[i][1] * view[7:15, :] + tap[i][2] * view[6:14, :])
-    cot_next = jnp.where(last, 0.0, after[3].astype(F32)[0:8])
-    x_next = (short[1] * short[2]).astype(BF16).astype(F32)[0:2]
-    g_next = (cot_next * short[0]).astype(BF16).astype(F32)[0:1]
-    h0 = over(wn_j)
-    h1 = over(wn_j * less)
-    long0 = over(wn_j * less * sout[0]) + h0 * x_next[0:1]
-    long1 = over(wn_j * less * less * sout[0]) + h1 * x_next[0:1] + h0 * x_next[1:2]
-    gg0 = over(wn_j * one * gin[0])
-    gg1 = over(wn_j * one * one * gin[0]) - over(wn_j * one) * g_next
-    row8 = row_iota(8)
-    long_next = jnp.where(row8 == 0, long0, jnp.where(row8 == 1, long1, 0.0))
-    gg_next = jnp.where(row8 == 0, gg0, jnp.where(row8 == 1, gg1, 0.0))
-    ef[0, length : length + 8, :] = cot_next * long_next
-    ef[1, length : length + 8, :] = gg_next * short[2]
-    ef[2, length : length + 8, :] = gg_next * short[1]
-
-    size = 32
+    size = 64
 
     def spread(c, _):
         base = pl.multiple_of(length - size - c * size, size)
@@ -471,16 +491,15 @@
     vmem = pl.BlockSpec(memory_space=pltpu.VMEM)
     dma = pltpu.SemaphoreType.DMA
     shape = jax.ShapeDtypeStruct
-    natural = shape((tiles, modes, LANES), F32)
+    edge = shape((tiles, 3, 8, LANES), F32)
     tokens3 = shape((tiles, length, LANES), BF16)
     middle = pl.pallas_call(
         functools.partial(filters_kernel, n, tiles, halves, length, modes),
         out_shape=(
-            tokens3, tokens3, shape((3, 16, width), BF16), shape((4, 16, width), BF16),
-            natural, natural, natural, natural, shape((tiles, 16, LANES), F32), shape((modes, LANES), F32),
+            tokens3, tokens3, edge, edge, shape((tiles, 16, LANES), F32), shape((modes, LANES), F32),
         ),
         in_specs=[hbm] * 4 + [vmem] * 3,
-        out_specs=[hbm] * 2 + [vmem] * 8,
+        out_specs=[hbm] * 2 + [vmem] * 4,
         scratch_shapes=[
             pltpu.VMEM((4, tiles, length, LANES), BF16),
             pltpu.VMEM((tiles, 3, length + 16, LANES), F32),
@@ -504,6 +523,10 @@
             pltpu.VMEM((2, 2, length, LANES), BF16),
             pltpu.VMEM((tiles, 16, LANES), F32),
             pltpu.VMEM((groups, modes, LANES), F32),
+            pltpu.VMEM((tiles, modes, LANES), F32),
+            pltpu.VMEM((tiles, modes, LANES), F32),
+            pltpu.VMEM((tiles, modes, LANES), F32),
+            pltpu.VMEM((tiles, modes, LANES), F32),
             pltpu.VMEM((n, 2 * modes + 16 * cut, LANES), BF16),
             pltpu.VMEM((n, 16 * (tiles - cut), LANES), BF16),
             dma((4, tiles)), dma((7,)), dma((7,)), dma((halves, n)), dma((halves, n)), dma((2, 2)),
@@ -522,14 +545,14 @@
 
     tokens = pl.BlockSpec((length, LANES), lambda j: (0, j))
     big = shape((length, width), BF16)
-    state = stack(1, modes, LANES)
+    edges = pl.BlockSpec((1, 3, 8, LANES), lambda j: (j, 0, 0, 0))
     *grads, grad_res = pl.pallas_call(
-        functools.partial(outputs_kernel, n, length, groups),
+        functools.partial(outputs_kernel, length, groups),
         grid=(tiles,),
         out_shape=(big, big, big, big, shape((3, 3, width), F32), shape((modes, groups), F32)),
         in_specs=[
             tokens, tokens, tokens, tokens, wide(3, 3, LANES), stack(1, length, LANES), stack(1, length, LANES),
-            wide(3, 16, LANES), wide(4, 16, LANES), state, state, state, state, stack(1, 16, LANES),
+            edges, edges, stack(1, 16, LANES),
             pl.BlockSpec((modes, LANES), lambda j: (0, 0)),
         ],
         out_specs=[tokens] * 4 + [wide(3, 3, LANES), pl.BlockSpec((modes, groups), lambda j: (0, 0))],

time: 66.9 us -> 64.5 us (0.964)
  Pallas kernels: 65.8 us -> 63.5 us
    pallas_call x1, Pallas kernels: 51.9 us -> 50 us  [local(): pl.pallas_call(functools.partial(filters_kernel, n, tiles, halves, length...]
where the time goes in v4:
time: 64.5 us; the launch traced here: 64.1 us
  Pallas kernels  63.5 us (98%)
    pallas_call x1, Pallas kernels, local(): pl.pallas_call(functools.partial(filters_kernel, n, tiles, halves, length...  50 us
    pallas_call x1, Pallas kernels, local(): pl.pallas_call(functools.partial(outputs_kernel, length, groups), grid=(t...  13.5 us

profile of v4, /device:TPU:1, one launch (start us, length us, event | category | flops | bytes accessed | tf_op | source)
XLA Modules:
  0.0 64.1 jit_solution(13578511884115853055)
XLA Ops:
  0.6 50.0 %shard_map.118 = (bf16[8,1024,128]{2,1,0:T(8,128)(2,1)}, bf16[8,1024,128]{2,1,0:T(8,128)(2,1)}, f32[8,3,8,128]{3,2,1,0:T(8,128)}, f32[8,3,8,128]{3,2,1,0:T(8,128...) custom-call(bf16[1024,1024]{1,0:T(8,128)(2,1)} %query.3, bf16[1024,1024]{1,0:T(8,128)(2,1)} %key.3, ...), custom_call_target="tpu_custom_call" | custom-call | tf_op jit(solution)/shard_map/pallas_call | solution.py:496
  50.7 13.5 %shard_map.119 = (bf16[1024,1024]{1,0:T(8,128)(2,1)}, bf16[1024,1024]{1,0:T(8,128)(2,1)}, bf16[1024,1024]{1,0:T(8,128)(2,1)}, bf16[1024,1024]{1,0:T(8,128)(2,1)}...) custom-call(bf16[1024,1024]{1,0:T(8,128)(2,1)} %query.3, bf16[1024,1024]{1,0:T(8,128)(2,1)} %key.3, bf16[1024,1024]{1,0:T(8,128)(2,1)} %value.3, ...), custom_call_target="tpu_custom_call" | custom-call | tf_op jit(solution)/shard_map/pallas_call | solution.py:549

commit v5 on v4

--- a/solution.py
+++ b/solution.py
@@ -122,7 +122,7 @@
                 ref[at, :, BLK : 2 * BLK] = left
         return 0
 
-    lax.fori_loop(0, tiles // 2, build, 0)
+    lax.fori_loop(0, tiles // 2, build, 0, unroll=2)
     pl.semaphore_wait(barrier, n - 1)
 
     def behind(i):
@@ -144,7 +144,7 @@
     for i in range(4):
         ahead(i).start()
 
-    lax.fori_loop(tiles // 2, tiles, build, 0)
+    lax.fori_loop(tiles // 2, tiles, build, 0, unroll=2)
 
     def arrive(j, _):
         for i in range(4):
@@ -184,7 +184,7 @@
         return gate
 
     def gates(j, _):
-        lax.fori_loop(1, BLK // 16, gate_of(j), 0)
+        lax.fori_loop(1, BLK // 16, gate_of(j), 0, unroll=7)
         return 0
 
     lax.fori_loop(0, tiles, gates, 0)
@@ -261,7 +261,7 @@
         gacc[...] = total
         return 0
 
-    lax.fori_loop(0, tiles, within, 0)
+    lax.fori_loop(0, tiles, within, 0, unroll=2)
 
     def combine(j, h):
         jj = j - h * per
@@ -344,7 +344,7 @@
                 stage[slot, 1, rows, :] = backs[b].astype(BF16)
             return tuple(sums)
 
-        sums = lax.fori_loop(0, BLK // 16, finish, (jnp.zeros((8, LANES), F32),) * 9)
+        sums = lax.fori_loop(0, BLK // 16, finish, (jnp.zeros((8, LANES), F32),) * 9, unroll=4)
         for at in range(9):
             tsum[j, at : at + 1, :] = jnp.sum(sums[at], axis=0, keepdims=True)
         tsum[j, 9:16, :] = jnp.zeros((7, LANES), F32)
@@ -474,7 +474,7 @@
             (grad_q, grad_k, grad_v)[i][rows, :] = total.astype(BF16)
         return 0
 
-    lax.fori_loop(0, length // size, spread, 0)
+    lax.fori_loop(0, length // size, spread, 0, unroll=4)
     for i in range(3):
         grad_taps[i] = taps_sum[0, 3 * i : 3 * i + 3, :]
     grad_res[...] = res_sum[:, 0:groups]

time: 64.5 us -> 59.6 us (0.924)
  Pallas kernels: 63.5 us -> 58.6 us
    pallas_call x1, Pallas kernels: 50 us -> 45.5 us  [local(): pl.pallas_call(functools.partial(filters_kernel, n, tiles, halves, length...]
where the time goes in v5:
time: 59.6 us; the launch traced here: 59.2 us
  Pallas kernels  58.6 us (98%)
  between operations  0.64 us (1%)
    pallas_call x1, Pallas kernels, local(): pl.pallas_call(functools.partial(filters_kernel, n, tiles, halves, length...  45.5 us
    pallas_call x1, Pallas kernels, local(): pl.pallas_call(functools.partial(outputs_kernel, length, groups), grid=(t...  13 us

profile of v5, /device:TPU:1, one launch (start us, length us, event | category | flops | bytes accessed | tf_op | source)
XLA Modules:
  0.0 59.2 jit_solution(15591393290083664051)
XLA Ops:
  0.6 45.5 %shard_map.118 = (bf16[8,1024,128]{2,1,0:T(8,128)(2,1)}, bf16[8,1024,128]{2,1,0:T(8,128)(2,1)}, f32[8,3,8,128]{3,2,1,0:T(8,128)}, f32[8,3,8,128]{3,2,1,0:T(8,128...) custom-call(bf16[1024,1024]{1,0:T(8,128)(2,1)} %query.3, bf16[1024,1024]{1,0:T(8,128)(2,1)} %key.3, ...), custom_call_target="tpu_custom_call" | custom-call | tf_op jit(solution)/shard_map/pallas_call | solution.py:496
  46.2 13.0 %shard_map.119 = (bf16[1024,1024]{1,0:T(8,128)(2,1)}, bf16[1024,1024]{1,0:T(8,128)(2,1)}, bf16[1024,1024]{1,0:T(8,128)(2,1)}, bf16[1024,1024]{1,0:T(8,128)(2,1)}...) custom-call(bf16[1024,1024]{1,0:T(8,128)(2,1)} %query.3, bf16[1024,1024]{1,0:T(8,128)(2,1)} %key.3, bf16[1024,1024]{1,0:T(8,128)(2,1)} %value.3, ...), custom_call_target="tpu_custom_call" | custom-call | tf_op jit(solution)/shard_map/pallas_call | solution.py:549

commit v6 on v5

--- a/solution.py
+++ b/solution.py
@@ -156,7 +156,7 @@
                 uf[j, i, pl.ds(pl.multiple_of(c * 64 + 8, 8), 64), :] = inb[i, j, rows, :].astype(F32)
             return 0
 
-        lax.fori_loop(0, length // 64, widen, 0)
+        lax.fori_loop(0, length // 64, widen, 0, unroll=4)
         return 0
 
     lax.fori_loop(0, tiles, arrive, 0)
@@ -450,7 +450,7 @@
             uf[i, pl.ds(pl.multiple_of(c * 64 + 8, 8), 64), :] = streams[i][rows, :].astype(F32)
         return 0
 
-    lax.fori_loop(0, length // 64, widen, 0)
+    lax.fori_loop(0, length // 64, widen, 0, unroll=4)
     tap = [[taps[i, l : l + 1, :] for l in range(3)] for i in range(3)]
 
     size = 64

time: 59.6 us -> 58.9 us (0.988)
  Pallas kernels: 58.6 us -> 57.9 us
where the time goes in v6:
time: 58.9 us; the launch traced here: 58.6 us
  Pallas kernels  57.9 us (98%)
  between operations  0.64 us (1%)
    pallas_call x1, Pallas kernels, local(): pl.pallas_call(functools.partial(filters_kernel, n, tiles, halves, length...  45.1 us
    pallas_call x1, Pallas kernels, local(): pl.pallas_call(functools.partial(outputs_kernel, length, groups), grid=(t...  12.8 us

profile of v6, /device:TPU:1, one launch (start us, length us, event | category | flops | bytes accessed | tf_op | source)
XLA Modules:
  0.0 58.6 jit_solution(1022682544334563601)
XLA Ops:
  0.6 45.1 %shard_map.118 = (bf16[8,1024,128]{2,1,0:T(8,128)(2,1)}, bf16[8,1024,128]{2,1,0:T(8,128)(2,1)}, f32[8,3,8,128]{3,2,1,0:T(8,128)}, f32[8,3,8,128]{3,2,1,0:T(8,128...) custom-call(bf16[1024,1024]{1,0:T(8,128)(2,1)} %query.3, bf16[1024,1024]{1,0:T(8,128)(2,1)} %key.3, ...), custom_call_target="tpu_custom_call" | custom-call | tf_op jit(solution)/shard_map/pallas_call | solution.py:496
  45.7 12.8 %shard_map.119 = (bf16[1024,1024]{1,0:T(8,128)(2,1)}, bf16[1024,1024]{1,0:T(8,128)(2,1)}, bf16[1024,1024]{1,0:T(8,128)(2,1)}, bf16[1024,1024]{1,0:T(8,128)(2,1)}...) custom-call(bf16[1024,1024]{1,0:T(8,128)(2,1)} %query.3, bf16[1024,1024]{1,0:T(8,128)(2,1)} %key.3, bf16[1024,1024]{1,0:T(8,128)(2,1)} %value.3, ...), custom_call_target="tpu_custom_call" | custom-call | tf_op jit(solution)/shard_map/pallas_call | solution.py:549
